TPU v7x, 32 devices: a whole 2x2x4 slice. The times are simulated.
32 devices in a mesh: dp: 4 (over z), fsdp: 8 (over y, x, core).
Axes of the slice: x: 2, y: 2, z: 4, core: 2. Of those that a mesh axis runs over, the one named last changes fastest.
Arguments:
- latents: bfloat16 [32, 320, 16], P(('dp', 'fsdp')), may hold values from -6 to 6
- noise: float32 [32, 320, 16], P(('dp', 'fsdp')), may hold values from -6 to 6
- lengths: int32 [32], P(('dp', 'fsdp')), may hold values from 192 to 320, as said below
- timesteps: int32 [32], P(('dp', 'fsdp')), may hold values from 0 to 999
- labels: int32 [32], P(('dp', 'fsdp')), may hold values from 0 to 1000
- enc_feats: float32 [32, 768], P(('dp', 'fsdp')), may hold values from -6 to 6
- pair_idx: int32 [32], P(('dp', 'fsdp')), may hold values from 0 to 31
- step: int32 [1], replicated, may hold values from 2 to 20
- rows_w: float32 [3, 9216, 1152], P(None, ('dp', 'fsdp'))
- fc2_w: float32 [3, 4608, 1152], P(None, ('dp', 'fsdp')), may hold values from -0.09375 to 0.09375
- misc_w: float32 [5101056], P(('dp', 'fsdp'))
- gains: float32 [16128], P(('dp', 'fsdp'))
- rows_m: float32 [3, 9216, 1152], P(None, ('dp', 'fsdp')), may hold values from -2.3841858e-06 to 2.3841858e-06
- rows_v: float32 [3, 9216, 1152], P(None, ('dp', 'fsdp')), may hold values from 1.0020243e-13 to 3.970285e-13
- fc2_m: float32 [3, 4608, 1152], P(None, ('dp', 'fsdp')), may hold values from -2.3841858e-06 to 2.3841858e-06
- fc2_v: float32 [3, 4608, 1152], P(None, ('dp', 'fsdp')), may hold values from 1.0020243e-13 to 3.970285e-13
- misc_m: float32 [5101056], P(('dp', 'fsdp')), may hold values from -2.3841858e-06 to 2.3841858e-06
- misc_v: float32 [5101056], P(('dp', 'fsdp')), may hold values from 3.0249791e-12 to 1.20999166e-11
- gains_m: float32 [16128], P(('dp', 'fsdp')), may hold values from -2.2888184e-05 to 2.2888184e-05
- gains_v: float32 [16128], P(('dp', 'fsdp')), may hold values from 1.0020243e-11 to 3.970285e-11
Outputs:
- loss: float32 [], replicated
- grad_norm: float32 [], replicated
- rows_new: float32 [3, 9216, 1152], P(None, ('dp', 'fsdp'))
- rows_m_new: float32 [3, 9216, 1152], P(None, ('dp', 'fsdp'))
- rows_v_new: float32 [3, 9216, 1152], P(None, ('dp', 'fsdp'))
- rows_low: bfloat16 [3, 9216, 1152], P(None, ('dp', 'fsdp'))
- fc2_new: float32 [3, 4608, 1152], P(None, ('dp', 'fsdp'))
- fc2_m_new: float32 [3, 4608, 1152], P(None, ('dp', 'fsdp'))
- fc2_v_new: float32 [3, 4608, 1152], P(None, ('dp', 'fsdp'))
- fc2_low: bfloat16 [3, 4608, 1152], P(None, ('dp', 'fsdp'))
- misc_new: float32 [5101056], P(('dp', 'fsdp'))
- misc_m_new: float32 [5101056], P(('dp', 'fsdp'))
- misc_v_new: float32 [5101056], P(('dp', 'fsdp'))
- misc_low: bfloat16 [5101056], P(('dp', 'fsdp'))
- gains_new: float32 [16128], P(('dp', 'fsdp'))
- gains_m_new: float32 [16128], P(('dp', 'fsdp'))
- gains_v_new: float32 [16128], P(('dp', 'fsdp'))
- gains_low: bfloat16 [16128], P(('dp', 'fsdp'))
- norms: float32 [19, 2], replicated
Inputs may be any that keep to these rules, and one draw needn't show every extreme that they name: `lengths`: live patches of an item; patch slot j is live where j < the length; in every draw some item has 320 and another 192.
All inputs are finite; a program needn't handle non-finite values.
Results may differ from a plain program's by a relative error of at most 0.012.
The roundings to bfloat16 on the way count: a program that leaves them out, or rounds other values in their place, can miss the bound.
Values may be sent and summed in bfloat16 or wider, within the bound.
A program may use at most 576 MiB of HBM per device.

v0:
```python
import math

import jax
import jax.numpy as jnp
from jax import lax
from jax.sharding import PartitionSpec as P

D = 1152
H = 16
HD = 72
PIN = 16
ENC = 768
CLS = 1001
L = 322
BLOCKS = 3
PATCH = 320


logit_softening_scale = 0.02
align_weight = 0.5
clip_limit = 0.01
beta_first = 0.9
beta_second = 0.95
learn_rate = 0.3
weight_decay = 0.01
adam_eps = 1e-08
layer_eps = 1e-05
vector_eps = 1e-06
mask_fill = -1e30


def misc_bounds():
    return [(PIN + 1) * D, D * PIN, L * D, CLS * D, 2 * D * D, D * ENC]


def split_misc(flat):
    shapes = [(PIN + 1, D), (D, PIN), (L, D), (CLS, D), (2 * D, D), (D, ENC)]
    pieces = []
    offset = 0
    for shape_now in shapes:
        length = shape_now[0] * shape_now[1]
        pieces.append(flat[offset : offset + length].reshape(shape_now))
        offset += length
    return pieces


def time_embed(timesteps):
    half_width = D // 2
    frequency = jnp.exp(
        -math.log(10000.0) * jnp.arange(half_width).astype(jnp.float32) / half_width
    )
    angles = timesteps.astype(jnp.float32)[:, None] * frequency[None, :]
    return jnp.concatenate([jnp.cos(angles), jnp.sin(angles)], axis=-1)


def collected_sample_embeddings(left, right):
    return lax.dot_general(
        left.reshape(-1, left.shape[-1]),
        right.reshape(-1, right.shape[-1]),
        (((0,), (0,)), ((), ())),
        preferred_element_type=jnp.float32,
    )


def gram_crossing(left, right):
    return lax.dot_general(
        left, right, (((left.ndim - 1,), (1,)), ((), ())), preferred_element_type=jnp.float32
    )


def layer_norm(values, gain, bias):
    centered = values - jnp.mean(values, axis=-1, keepdims=True)
    scale_inv = lax.rsqrt(jnp.mean(centered * centered, axis=-1, keepdims=True) + layer_eps)
    normal = centered * scale_inv
    return (normal * gain + bias, (normal, scale_inv))


def norm_back(grad, saved, gain):
    normal, scale_inv = saved
    dnormal = grad * gain
    dvalues = scale_inv * (
        dnormal
        - jnp.mean(dnormal, axis=-1, keepdims=True)
        - normal * jnp.mean(dnormal * normal, axis=-1, keepdims=True)
    )
    dgain = jnp.sum((grad * normal).reshape(-1, grad.shape[-1]), axis=0)
    dbias = jnp.sum(grad.reshape(-1, grad.shape[-1]), axis=0)
    return (dvalues, dgain, dbias)


def split_heads(triple):
    shaped = triple.reshape(triple.shape[0], triple.shape[1], 3, H, HD)
    return (shaped[:, :, 0], shaped[:, :, 1], shaped[:, :, 2])


def attend_scores(queries, keys_all, keymask):
    scores = jnp.einsum(
        "ilhd,imhd->ihlm", queries, keys_all, preferred_element_type=jnp.float32
    ) * HD ** (-0.5)
    return jnp.where(keymask[:, None, None, :], scores, mask_fill)


def attend_forward(triple, keymask):
    queries, keys_all, values = split_heads(triple)
    scores = attend_scores(queries, keys_all, keymask)
    highest = jnp.max(scores, axis=-1, keepdims=True)
    logsum = highest + jnp.log(jnp.sum(jnp.exp(scores - highest), axis=-1, keepdims=True))
    probs = jnp.exp(scores - logsum).astype(jnp.bfloat16)
    attended = jnp.einsum("ihlm,imhd->ilhd", probs, values, preferred_element_type=jnp.float32)
    return (attended.reshape(triple.shape[0], triple.shape[1], H * HD).astype(jnp.bfloat16), logsum)


def attend_backward(dattended, triple, logsum, keymask):
    queries, keys_all, values = split_heads(triple)
    probs = jnp.exp(attend_scores(queries, keys_all, keymask) - logsum)
    dout = dattended.reshape(dattended.shape[0], dattended.shape[1], H, HD)
    dprobs = jnp.einsum("ilhd,imhd->ihlm", dout, values, preferred_element_type=jnp.float32)
    dscores = (probs * (dprobs - jnp.sum(probs * dprobs, axis=-1, keepdims=True))).astype(
        jnp.bfloat16
    )
    dqueries = jnp.einsum(
        "ihlm,imhd->ilhd", dscores, keys_all, preferred_element_type=jnp.float32
    ) * HD ** (-0.5)
    dkeys = jnp.einsum(
        "ihlm,ilhd->imhd", dscores, queries, preferred_element_type=jnp.float32
    ) * HD ** (-0.5)
    dvalues = jnp.einsum(
        "ihlm,ilhd->imhd", probs.astype(jnp.bfloat16), dout, preferred_element_type=jnp.float32
    )
    joined = jnp.stack([dqueries, dkeys, dvalues], axis=2)
    return joined.reshape(triple.shape).astype(jnp.bfloat16)


def block_forward(hidden, rows, fc2, gvec, keymask):
    normed, save_one = layer_norm(hidden, gvec[0], gvec[1])
    normed_low = normed.astype(jnp.bfloat16)
    triple = gram_crossing(normed_low, rows[: 3 * D]).astype(jnp.bfloat16)
    attended, logsum = attend_forward(triple, keymask)
    after = hidden + gram_crossing(attended, rows[3 * D : 4 * D])
    normed_two, save_two = layer_norm(after, gvec[2], gvec[3])
    normed_two_low = normed_two.astype(jnp.bfloat16)
    inner = gram_crossing(normed_two_low, rows[4 * D :])
    active = jax.nn.gelu(inner, approximate=True).astype(jnp.bfloat16)
    output = after + jnp.dot(active, fc2, preferred_element_type=jnp.float32)
    return (
        output,
        (save_one, normed_low, triple, logsum, attended, save_two, normed_two_low, inner, active),
    )


def block_backward(dout, rows, fc2, gvec, keymask, saved):
    save_one, normed_low, triple, logsum, attended, save_two, normed_two_low, inner, active = saved
    dlow = dout.astype(jnp.bfloat16)
    grad_fc2 = collected_sample_embeddings(active, dlow)
    dactive = gram_crossing(dlow, fc2)
    slope = jax.vjp(lambda entry: jax.nn.gelu(entry, approximate=True), inner)[1](dactive)[0]
    dinner = slope.astype(jnp.bfloat16)
    grad_first = collected_sample_embeddings(dinner, normed_two_low)
    dnormed_two = jnp.dot(dinner, rows[4 * D :], preferred_element_type=jnp.float32)
    dafter_norm, dgain_two, dbias_two = norm_back(dnormed_two, save_two, gvec[2])
    dafter = dout + dafter_norm
    dafter_low = dafter.astype(jnp.bfloat16)
    grad_out = collected_sample_embeddings(dafter_low, attended)
    dattended = jnp.dot(dafter_low, rows[3 * D : 4 * D], preferred_element_type=jnp.float32).astype(
        jnp.bfloat16
    )
    dtriple = attend_backward(dattended, triple, logsum, keymask)
    grad_triple = collected_sample_embeddings(dtriple, normed_low)
    dnormed = jnp.dot(dtriple, rows[: 3 * D], preferred_element_type=jnp.float32)
    dhidden_norm, dgain_one, dbias_one = norm_back(dnormed, save_one, gvec[0])
    grad_rows = jnp.concatenate([grad_triple, grad_out, grad_first], axis=0)
    gain_grad = jnp.stack([dgain_one, dbias_one, dgain_two, dbias_two])
    return (dafter + dhidden_norm, grad_rows, grad_fc2, gain_grad)


def segment_kinds(rank_here, cols_here, misc_here):
    column = rank_here * cols_here + jnp.arange(cols_here)
    column_kind = (column >= 3 * D).astype(jnp.int32) + (column >= 4 * D).astype(jnp.int32)
    flat_index = rank_here * misc_here + jnp.arange(misc_here)
    misc_kind = jnp.zeros((misc_here,), jnp.int32)
    offset = 0
    for length in misc_bounds()[:-1]:
        offset += length
        misc_kind = misc_kind + (flat_index >= offset).astype(jnp.int32)
    return (column_kind, misc_kind)


def squares(kinds, rows, fc2, misc, gain_flat):
    column_kind, misc_kind = kinds
    column_sums = jnp.sum(rows * rows, axis=2)
    rows_part = jnp.stack(
        [
            jnp.sum(jnp.where(column_kind == segment, column_sums, 0.0), axis=1)
            for segment in range(3)
        ],
        axis=1,
    ).reshape(-1)
    fc2_part = jnp.sum(fc2 * fc2, axis=(1, 2))
    misc_part = jnp.stack(
        [jnp.sum(jnp.where(misc_kind == segment, misc * misc, 0.0)) for segment in range(6)]
    )
    return jnp.concatenate([rows_part, fc2_part, misc_part, jnp.sum(gain_flat * gain_flat)[None]])


def spread(ratios, kinds, blocks):
    column_kind, misc_kind = kinds
    rows_map = ratios[3 * jnp.arange(blocks)[:, None, None] + column_kind[None, :, None]]
    fc2_map = ratios[3 * blocks + jnp.arange(blocks)][:, None, None]
    misc_map = ratios[4 * blocks + misc_kind]
    return (rows_map, fc2_map, misc_map, ratios[4 * blocks + 6])


def adam_move(grad, weight, first, second, factor, count, decay_now):
    clipped = factor * grad
    first_new = beta_first * first + (1.0 - beta_first) * clipped
    second_new = beta_second * second + (1.0 - beta_second) * clipped * clipped
    first_hat = first_new / (1.0 - beta_first**count)
    second_hat = second_new / (1.0 - beta_second**count)
    return (
        first_new,
        second_new,
        first_hat / (jnp.sqrt(second_hat) + adam_eps) + decay_now * weight,
    )


def local(
    latents,
    noise,
    lengths,
    timesteps,
    labels,
    enc_feats,
    pair_idx,
    step,
    rows_w,
    fc2_w,
    misc_w,
    gains,
    rows_m,
    rows_v,
    fc2_m,
    fc2_v,
    misc_m,
    misc_v,
    gains_m,
    gains_v,
):
    rank_here = lax.axis_index(("dp", "fsdp"))
    count_items = latents.shape[0]
    total_items = count_items * lax.axis_size(("dp", "fsdp"))
    rows_all, fc2_all, misc_all, gains_all = (
        lax.all_gather(rows_w.astype(jnp.bfloat16), ("dp", "fsdp"), axis=1, tiled=True),
        lax.all_gather(fc2_w.astype(jnp.bfloat16), ("dp", "fsdp"), axis=1, tiled=True),
        lax.all_gather(misc_w.astype(jnp.bfloat16), ("dp", "fsdp"), axis=0, tiled=True),
        lax.all_gather(gains.astype(jnp.bfloat16), ("dp", "fsdp"), axis=0, tiled=True),
    )
    embed, head, posit, table, skip, align = split_misc(misc_all)
    gain_rows = gains_all.astype(jnp.float32).reshape(-1, D)
    keymask = jnp.arange(L)[None, :] < lengths[:, None] + 2
    valid = (jnp.arange(PATCH)[None, :] < lengths[:, None]).astype(jnp.float32)
    live_count = lengths.astype(jnp.float32)
    patches = jnp.dot(latents, embed[:PIN], preferred_element_type=jnp.float32) + embed[PIN].astype(
        jnp.float32
    )
    class_rows = jnp.take(table, labels, axis=0).astype(jnp.float32)
    hidden = jnp.concatenate([time_embed(timesteps)[:, None], class_rows[:, None], patches], axis=1)
    hidden = hidden + posit.astype(jnp.float32)[None]
    saved_all = []
    outputs = []
    for block_id in range(BLOCKS):
        if block_id == BLOCKS - 1:
            joined = jnp.concatenate([hidden, outputs[0]], axis=-1).astype(jnp.bfloat16)
            hidden = jnp.dot(joined, skip, preferred_element_type=jnp.float32)
        hidden, saved = block_forward(
            hidden,
            rows_all[block_id],
            fc2_all[block_id],
            gain_rows[4 * block_id : 4 * block_id + 4],
            keymask,
        )
        saved_all.append(saved)
        outputs.append(hidden)
    final, save_final = layer_norm(hidden[:, 2:], gain_rows[12], gain_rows[13])
    final_low = final.astype(jnp.bfloat16)
    pred = jnp.dot(final_low, head, preferred_element_type=jnp.float32)
    denom = live_count * PIN
    diff = (pred - noise) * valid[:, :, None]
    mse_local = jnp.sum(jnp.sum(diff * diff, axis=(1, 2)) / denom) / total_items
    dpred = (2.0 * diff / denom[:, None, None] / total_items).astype(jnp.bfloat16)
    grad_head = collected_sample_embeddings(final_low, dpred)
    dfinal, dgain_final, dbias_final = norm_back(
        gram_crossing(dpred, head), save_final, gain_rows[12]
    )
    middle = outputs[1]
    pooled_low = (jnp.sum(middle[:, 2:] * valid[:, :, None], axis=1) / live_count[:, None]).astype(
        jnp.bfloat16
    )
    projected = jnp.dot(pooled_low, align, preferred_element_type=jnp.float32)
    inverse = lax.rsqrt(jnp.sum(projected * projected, axis=-1, keepdims=True) + vector_eps)
    zhat = projected * inverse
    whole_embedding_table = lax.all_gather(
        zhat.astype(jnp.bfloat16), ("dp", "fsdp"), axis=0, tiled=True
    )
    normalised_latent_embeddings = (
        enc_feats * lax.rsqrt(jnp.sum(enc_feats * enc_feats, axis=-1, keepdims=True) + vector_eps)
    ).astype(jnp.bfloat16)
    cosine_score_table = (
        gram_crossing(normalised_latent_embeddings, whole_embedding_table) / logit_softening_scale
    )
    highest = jnp.max(cosine_score_table, axis=-1, keepdims=True)
    logsum = highest + jnp.log(
        jnp.sum(jnp.exp(cosine_score_table - highest), axis=-1, keepdims=True)
    )
    target = (jnp.arange(total_items)[None, :] == pair_idx[:, None]).astype(jnp.float32)
    align_local = (
        jnp.sum(logsum[:, 0] - jnp.sum(target * cosine_score_table, axis=-1)) / total_items
    )
    cosine_score_derivative = (
        (jnp.exp(cosine_score_table - logsum) - target) * (align_weight / total_items)
    ).astype(jnp.bfloat16)
    feature_set_gradient = (
        collected_sample_embeddings(cosine_score_derivative, normalised_latent_embeddings)
        / logit_softening_scale
    )
    dzhat = lax.psum_scatter(feature_set_gradient, ("dp", "fsdp"), scatter_dimension=0, tiled=True)
    dproj = (inverse * (dzhat - zhat * jnp.sum(dzhat * zhat, axis=-1, keepdims=True))).astype(
        jnp.bfloat16
    )
    grad_align = collected_sample_embeddings(pooled_low, dproj)
    dpooled = gram_crossing(dproj, align)
    dmid_extra = jnp.concatenate(
        [
            jnp.zeros((count_items, 2, D), jnp.float32),
            valid[:, :, None] * dpooled[:, None, :] / live_count[:, None, None],
        ],
        axis=1,
    )
    dhidden = jnp.concatenate([jnp.zeros((count_items, 2, D), jnp.float32), dfinal], axis=1)
    rows_grads = [None] * BLOCKS
    fc2_grads = [None] * BLOCKS
    gain_grads = [None] * BLOCKS
    first_rows_full = None
    first_fc2_full = None
    dshort = None
    grad_skip = None
    for block_id in range(BLOCKS - 1, -1, -1):
        rows_now, fc2_now = (rows_all[block_id], fc2_all[block_id])
        dhidden, grad_rows_full, grad_fc2_full, gain_grads[block_id] = block_backward(
            dhidden,
            rows_now,
            fc2_now,
            gain_rows[4 * block_id : 4 * block_id + 4],
            keymask,
            saved_all[block_id],
        )
        if block_id > 0:
            rows_grads[block_id], fc2_grads[block_id] = (
                lax.psum_scatter(grad_rows_full, ("dp", "fsdp"), scatter_dimension=0, tiled=True),
                lax.psum_scatter(grad_fc2_full, ("dp", "fsdp"), scatter_dimension=0, tiled=True),
            )
        else:
            first_rows_full, first_fc2_full = (grad_rows_full, grad_fc2_full)
        if block_id == BLOCKS - 1:
            dlow = dhidden.astype(jnp.bfloat16)
            grad_skip = collected_sample_embeddings(joined, dlow)
            djoined = gram_crossing(dlow, skip)
            dhidden = djoined[..., :D] + dmid_extra
            dshort = djoined[..., D:]
        elif block_id == 1:
            dhidden = dhidden + dshort
    dpatch = dhidden[:, 2:]
    grad_embed = collected_sample_embeddings(latents, dpatch.astype(jnp.bfloat16))
    grad_patch_bias = jnp.sum(dpatch.reshape(-1, D), axis=0)
    grad_pos = jnp.sum(dhidden, axis=0)
    onehot = (labels[:, None] == jnp.arange(CLS)[None, :]).astype(jnp.float32)
    grad_table = jnp.dot(
        onehot.T, dhidden[:, 1], precision=lax.Precision.HIGHEST, preferred_element_type=jnp.float32
    )
    misc_grad = jnp.concatenate(
        [
            grad_embed.reshape(-1),
            grad_patch_bias,
            grad_head.reshape(-1),
            grad_pos.reshape(-1),
            grad_table.reshape(-1),
            grad_skip.reshape(-1),
            grad_align.reshape(-1),
        ]
    )
    gains_grad = jnp.concatenate(
        [gain_grads[0], gain_grads[1], gain_grads[2], jnp.stack([dgain_final, dbias_final])], axis=0
    ).reshape(-1)
    rows_grads[0], fc2_grads[0], misc_shard, gains_shard = (
        lax.psum_scatter(first_rows_full, ("dp", "fsdp"), scatter_dimension=0, tiled=True),
        lax.psum_scatter(first_fc2_full, ("dp", "fsdp"), scatter_dimension=0, tiled=True),
        lax.psum_scatter(misc_grad, ("dp", "fsdp"), scatter_dimension=0, tiled=True),
        lax.psum_scatter(gains_grad, ("dp", "fsdp"), scatter_dimension=0, tiled=True),
    )
    grads = (jnp.stack(rows_grads), jnp.stack(fc2_grads), misc_shard, gains_shard)
    weights = (rows_w, fc2_w, misc_w, gains)
    firsts = (rows_m, fc2_m, misc_m, gains_m)
    seconds = (rows_v, fc2_v, misc_v, gains_v)
    kinds = segment_kinds(rank_here, rows_w.shape[1], misc_w.shape[0])
    grad_squares, weight_squares, loss = lax.psum(
        (
            squares(kinds, grads[0], grads[1], grads[2], grads[3]),
            squares(kinds, rows_w, fc2_w, misc_w, gains),
            mse_local + align_weight * align_local,
        ),
        ("dp", "fsdp"),
    )
    grad_norm = jnp.sqrt(jnp.sum(grad_squares))
    factor = jnp.minimum(1.0, clip_limit / grad_norm)
    count = step[0].astype(jnp.float32)
    moved = [
        adam_move(
            grads[member],
            weights[member],
            firsts[member],
            seconds[member],
            factor,
            count,
            weight_decay if member < 3 else 0.0,
        )
        for member in range(4)
    ]
    updates = [entry[2] for entry in moved]
    update_squares = lax.psum(
        squares(kinds, updates[0], updates[1], updates[2], updates[3]), ("dp", "fsdp")
    )
    ratios = jnp.sqrt(weight_squares) / jnp.sqrt(update_squares + vector_eps)
    ratio_maps = spread(ratios, kinds, BLOCKS)
    renewed = [
        weights[member] - learn_rate * ratio_maps[member] * updates[member] for member in range(4)
    ]
    norms = jnp.stack([jnp.sqrt(weight_squares), jnp.sqrt(update_squares)], axis=1)
    return (
        loss,
        grad_norm,
        renewed[0],
        moved[0][0],
        moved[0][1],
        renewed[0].astype(jnp.bfloat16),
        renewed[1],
        moved[1][0],
        moved[1][1],
        renewed[1].astype(jnp.bfloat16),
        renewed[2],
        moved[2][0],
        moved[2][1],
        renewed[2].astype(jnp.bfloat16),
        renewed[3],
        moved[3][0],
        moved[3][1],
        renewed[3].astype(jnp.bfloat16),
        norms,
    )


def solution(mesh):
    in_specs = (
        P(("dp", "fsdp"), None, None),
        P(("dp", "fsdp"), None, None),
        P(("dp", "fsdp")),
        P(("dp", "fsdp")),
        P(("dp", "fsdp")),
        P(("dp", "fsdp"), None),
        P(("dp", "fsdp")),
        P(),
        P(None, ("dp", "fsdp"), None),
        P(None, ("dp", "fsdp"), None),
        P(("dp", "fsdp")),
        P(("dp", "fsdp")),
        P(None, ("dp", "fsdp"), None),
        P(None, ("dp", "fsdp"), None),
        P(None, ("dp", "fsdp"), None),
        P(None, ("dp", "fsdp"), None),
        P(("dp", "fsdp")),
        P(("dp", "fsdp")),
        P(("dp", "fsdp")),
        P(("dp", "fsdp")),
    )
    out_specs = (
        P(),
        P(),
        P(None, ("dp", "fsdp"), None),
        P(None, ("dp", "fsdp"), None),
        P(None, ("dp", "fsdp"), None),
        P(None, ("dp", "fsdp"), None),
        P(None, ("dp", "fsdp"), None),
        P(None, ("dp", "fsdp"), None),
        P(None, ("dp", "fsdp"), None),
        P(None, ("dp", "fsdp"), None),
        P(("dp", "fsdp")),
        P(("dp", "fsdp")),
        P(("dp", "fsdp")),
        P(("dp", "fsdp")),
        P(("dp", "fsdp")),
        P(("dp", "fsdp")),
        P(("dp", "fsdp")),
        P(("dp", "fsdp")),
        P(),
    )
    return jax.shard_map(local, mesh=mesh, in_specs=in_specs, out_specs=out_specs, check_vma=False)
```

profile of v0, /device:TPU:0, one launch (start us, length us, event | category | flops | bytes accessed | tf_op | source)
XLA Modules:
  0.0 3723.1 jit_solution(3150378448717236266)
XLA Ops:
  33.5 44.0 %all-reduce.3 = bf16[16128]{0:T(1024)(128)(2,1)S(1)} all-reduce(bf16[16128]{0:T(1024)(128)(2,1)S(1)} %dynamic-update-slice.2), channel_id=1, replica_groups=mesh['dp'=4,'fsdp'=8] {'dp','fsdp'}, use_global_device_ids=true, to_apply=%add.3 | all-reduce | flops 16128 | bytes 64512
  78.4 145.6 %all-reduce.12.cloned.1.call-done = bf16[5101056]{0:T(1024)(128)(2,1)} async-done(((bf16[5101056]{0:T(1024)(128)(2,1)}), bf16[5101056]{0:T(1024)(128)(2,1)}) %all-reduce.12.cloned.1.call-update) | async-done | bytes 10202128
  260.2 307.3 %all-gather.5.cloned.1.call-done = bf16[3,9216,1152]{2,1,0:T(8,128)(2,1)} async-done(((bf16[3,288,1152]{2,1,0:T(8,128)(2,1)}), bf16[3,9216,1152]{2,1,0:T(8,128)(2,1)}) %all-gather.5.cloned.1.call-update) | async-done | bytes 63701008 | tf_op jit(solution)/shard_map/all_gather | solution.py:252
  594.7 11.0 fusion.1
  605.6 150.3 %all-gather.7.cloned.1.call-done = bf16[3,4608,1152]{2,1,0:T(8,128)(2,1)} async-done(((bf16[3,144,1152]{2,1,0:T(8,128)(2,1)}), bf16[3,4608,1152]{2,1,0:T(8,128)(2,1)}) %all-gather.7.cloned.1.call-update) | async-done | bytes 31850512 | tf_op jit(solution)/shard_map/all_gather | solution.py:253
  799.9 11.9 fusion.187
  847.6 10.8 fusion.52
  929.9 38.8 %all-gather.1 = bf16[32,1,768]{2,1,0:T(2,128)(2,1)S(1)} all-gather(bf16[1,1,768]{2,1,0:T(2,128)(2,1)S(1)} %reshape.1891), channel_id=2, replica_groups=mesh['dp'=4,'fsdp'=8] {'dp','fsdp'}, dimensions={0}, use_global_device_ids=true | all-gather | bytes 50688 | tf_op jit(solution)/shard_map/all_gather | solution.py:301
  976.3 11.4 reshape.1762
  987.7 102.0 %all-reduce.14.cloned.1.call-done = f32[32,768]{1,0:T(8,128)} async-done(((f32[32,768]{1,0:T(8,128)}), f32[32,768]{1,0:T(8,128)}) %all-reduce.14.cloned.1.call-update) | async-done | bytes 98320
  1220.4 13.5 dynamic-update-slice.6
  1233.9 39.8 %dynamic-update-slice.7 = f32[5101056]{0:T(1024)} dynamic-update-slice(f32[5101056]{0:T(1024)} %dynamic-update-slice.6, f32[1153152]{0:T(1024)} %reshape.1761, s32[]{} %constant.321) | dynamic-update-slice | bytes 9225220
  1273.7 90.4 %dynamic-update-slice.8 = f32[5101056]{0:T(1024)} dynamic-update-slice(f32[5101056]{0:T(1024)} %dynamic-update-slice.7, f32[2654208]{0:T(1024)} %reshape.1762, s32[]{} %constant.322) | dynamic-update-slice | bytes 21233668
  1364.1 31.0 dynamic-update-slice.9
  1395.2 13.8 fusion.117
  1409.1 13.5 fusion.80
  1423.8 15.3 fusion.86
  1462.0 28.3 pad_maximum_fusion.2
  1512.5 28.5 pad_maximum_fusion
  1562.9 28.5 pad_maximum_fusion.1
  1640.3 42.0 %all-reduce.6 = f32[16128]{0:T(1024)S(1)} all-reduce(f32[16128]{0:T(1024)S(1)} %reshape.1764), channel_id=11, replica_groups=mesh['dp'=4,'fsdp'=8] {'dp','fsdp'}, use_global_device_ids=true, to_apply=%region_80.81.clone | all-reduce | flops 16128 | bytes 129024
  1682.9 36.8 all-reduce.16.cloned.1.call-done
  1722.3 223.6 %reduce-scatter.17.cloned.1.call-done = f32[144,1152]{1,0:T(8,128)} async-done(((f32[4608,1152]{1,0:T(8,128)}), f32[144,1152]{1,0:T(8,128)}) %reduce-scatter.17.cloned.1.call-update) | async-done | bytes 663568 | tf_op jit(solution)/shard_map/reduce_scatter | solution.py:359
  1945.9 226.7 %reduce-scatter.13.cloned.1.call-done = f32[144,1152]{1,0:T(8,128)} async-done(((f32[4608,1152]{1,0:T(8,128)}), f32[144,1152]{1,0:T(8,128)}) %reduce-scatter.13.cloned.1.call-update) | async-done | bytes 663568 | tf_op jit(solution)/shard_map/reduce_scatter | solution.py:395
  2172.6 225.5 %reduce-scatter.15.cloned.1.call-done = f32[144,1152]{1,0:T(8,128)} async-done(((f32[4608,1152]{1,0:T(8,128)}), f32[144,1152]{1,0:T(8,128)}) %reduce-scatter.15.cloned.1.call-update) | async-done | bytes 663568 | tf_op jit(solution)/shard_map/reduce_scatter | solution.py:359
  2399.9 383.7 %reduce-scatter.11.cloned.1.call-done = f32[288,1152]{1,0:T(8,128)} async-done(((f32[9216,1152]{1,0:T(8,128)}), f32[288,1152]{1,0:T(8,128)}) %reduce-scatter.11.cloned.1.call-update) | async-done | bytes 1327120 | tf_op jit(solution)/shard_map/reduce_scatter | solution.py:358
  2783.6 383.9 %reduce-scatter.7.cloned.1.call-done = f32[288,1152]{1,0:T(8,128)} async-done(((f32[9216,1152]{1,0:T(8,128)}), f32[288,1152]{1,0:T(8,128)}) %reduce-scatter.7.cloned.1.call-update) | async-done | bytes 1327120 | tf_op jit(solution)/shard_map/reduce_scatter | solution.py:394
  3167.5 385.6 %reduce-scatter.9.cloned.1.call-done = f32[288,1152]{1,0:T(8,128)} async-done(((f32[9216,1152]{1,0:T(8,128)}), f32[288,1152]{1,0:T(8,128)}) %reduce-scatter.9.cloned.1.call-update) | async-done | bytes 1327120 | tf_op jit(solution)/shard_map/reduce_scatter | solution.py:358
  3560.8 39.3 %psum.29 = f32[19]{0:T(128)S(1)} all-reduce(f32[19]{0:T(128)S(1)} %concatenate.73), channel_id=1, replica_groups=mesh['dp'=4,'fsdp'=8] {'dp','fsdp'}, use_global_device_ids=true, to_apply=%region_82.83 | all-reduce | flops 19 | bytes 152 | tf_op jit(solution)/shard_map/psum | solution.py:404
  3601.5 11.8 multiply_reduce_fusion.3
  3636.0 40.8 %all-reduce.7 = (f32[]{:T(128)}, f32[19]{0:T(128)S(1)}, f32[19]{0:T(128)S(1)}) all-reduce(f32[]{:T(128)} %bitcast.49, f32[19]{0:T(128)S(1)} %concatenate.75, f32[19]{0:T(128)S(1)} %concatenate.74), channel_id=1, replica_groups=mesh['dp'=4,'fsdp'=8] {'dp','fsdp'}, use_global_device_ids=true, to_apply=%region_27.28 | all-reduce | flops 39 | bytes 312 | tf_op jit(solution)/shard_map/psum | solution.py:404
  3694.7 11.3 fusion.103
  (637 shorter events, 549.2 us)
Async XLA Ops:
  7.2 250.5 %copy-start = (bf16[1,320,16]{1,2,0:T(8,128)(2,1)S(1)}, bf16[1,320,16]{1,2,0:T(8,128)(2,1)}, u32[]{:S(2)}) copy-start(bf16[1,320,16]{1,2,0:T(8,128)(2,1)} %param.20) | copy-start | bytes 30724
  7.2 216.8 %all-reduce.12.cloned.1.call-start = ((), (), s32[]{:S(2)}) async-start(), calls=%async_computation.14 | async-start | bytes 20406272
  20.3 547.2 %all-gather.5.cloned.1.call-start = ((), (), s32[]{:S(2)}) async-start(), calls=%async_computation.6 | async-start | bytes 65691648 | tf_op jit(solution)/shard_map/all_gather | solution.py:252
  26.2 729.8 %all-gather.7.cloned.1.call-start = ((), (), s32[]{:S(2)}) async-start(), calls=%async_computation.7 | async-start | bytes 32845824 | tf_op jit(solution)/shard_map/all_gather | solution.py:253
  28.1 1061.6 %all-reduce.14.cloned.1.call-start = ((), (), s32[]{:S(2)}) async-start(), calls=%async_computation.15 | async-start | bytes 196608
  78.3 489.2 %copy-start.97 = (f32[1152]{0:T(1024)}, f32[1152]{0:T(1024)S(1)}, u32[]{:S(2)}) copy-start(f32[1152]{0:T(1024)S(1)} %get-tuple-element.143) | copy-start | bytes 13828
  78.3 489.2 %copy-start.117 = (f32[1152]{0:T(1024)}, f32[1152]{0:T(1024)S(1)}, u32[]{:S(2)}) copy-start(f32[1152]{0:T(1024)S(1)} %get-tuple-element.144) | copy-start | bytes 13828
  78.3 516.3 %copy-start.94 = (f32[1152]{0:T(1024)}, f32[1152]{0:T(1024)S(1)}, u32[]{:S(2)}) copy-start(f32[1152]{0:T(1024)S(1)} %get-tuple-element.141) | copy-start | bytes 13828
  78.3 516.3 %copy-start.115 = (f32[1152]{0:T(1024)}, f32[1152]{0:T(1024)S(1)}, u32[]{:S(2)}) copy-start(f32[1152]{0:T(1024)S(1)} %get-tuple-element.142) | copy-start | bytes 13828
  78.3 688.6 %copy-start.91 = (f32[1152]{0:T(1024)}, f32[1152]{0:T(1024)S(1)}, u32[]{:S(2)}) copy-start(f32[1152]{0:T(1024)S(1)} %get-tuple-element.139) | copy-start | bytes 13828
  78.3 688.6 %copy-start.113 = (f32[1152]{0:T(1024)}, f32[1152]{0:T(1024)S(1)}, u32[]{:S(2)}) copy-start(f32[1152]{0:T(1024)S(1)} %get-tuple-element.140) | copy-start | bytes 13828
  78.3 713.9 %copy-start.88 = (f32[1152]{0:T(1024)}, f32[1152]{0:T(1024)S(1)}, u32[]{:S(2)}) copy-start(f32[1152]{0:T(1024)S(1)} %get-tuple-element.137) | copy-start | bytes 13828
  78.3 713.9 %copy-start.111 = (f32[1152]{0:T(1024)}, f32[1152]{0:T(1024)S(1)}, u32[]{:S(2)}) copy-start(f32[1152]{0:T(1024)S(1)} %get-tuple-element.138) | copy-start | bytes 13828
  78.4 736.1 %copy-start.121 = (f32[1152]{0:T(1024)}, f32[1152]{0:T(1024)S(1)}, u32[]{:S(2)}) copy-start(f32[1152]{0:T(1024)S(1)} %get-tuple-element.136) | copy-start | bytes 13828
  78.4 761.7 %copy-start.119 = (f32[1152]{0:T(1024)}, f32[1152]{0:T(1024)S(1)}, u32[]{:S(2)}) copy-start(f32[1152]{0:T(1024)S(1)} %get-tuple-element.134) | copy-start | bytes 13828
  78.4 804.5 %copy-start.99 = (f32[1152]{0:T(1024)}, f32[1152]{0:T(1024)S(1)}, u32[]{:S(2)}) copy-start(f32[1152]{0:T(1024)S(1)} %get-tuple-element.133) | copy-start | bytes 13828
  78.4 838.7 %copy-start.101 = (f32[1152]{0:T(1024)}, f32[1152]{0:T(1024)S(1)}, u32[]{:S(2)}) copy-start(f32[1152]{0:T(1024)S(1)} %get-tuple-element.135) | copy-start | bytes 13828
  259.9 330.8 %copy-start.5 = (f32[322,1152]{1,0:T(8,128)}, f32[322,1152]{1,0:T(8,128)S(1)}, u32[]{:S(2)}) copy-start(f32[322,1152]{1,0:T(8,128)S(1)} %get-tuple-element.123) | copy-start | bytes 4451332
  259.9 315.7 %copy-start.125 = (f32[322]{0:T(512)}, f32[322]{0:T(512)S(1)}, u32[]{:S(2)}) copy-start(f32[322]{0:T(512)S(1)} %broadcast_multiply_fusion.25) | copy-start | bytes 3868
  260.2 315.3 %copy-start.143 = (f32[322]{0:T(512)}, f32[322]{0:T(512)S(1)}, u32[]{:S(2)}) copy-start(f32[322]{0:T(512)S(1)} %add_rsqrt_fusion.6) | copy-start | bytes 3868
  594.3 161.7 %copy-start.21 = (f32[322,1152]{1,0:T(8,128)}, f32[322,1152]{1,0:T(8,128)S(1)}, u32[]{:S(2)}) copy-start(f32[322,1152]{1,0:T(8,128)S(1)} %get-tuple-element.174) | copy-start | bytes 4451332
  814.1 103.0 %copy-start.127 = (f32[322]{0:T(512)}, f32[322]{0:T(512)S(1)}, u32[]{:S(2)}) copy-start(f32[322]{0:T(512)S(1)} %broadcast_multiply_fusion.21) | copy-start | bytes 3868
  972.9 746.9 %all-reduce.16.cloned.1.call-start = ((), (), s32[]{:S(2)}) async-start(), calls=%async_computation.16 | async-start | bytes 40812544
  1395.2 550.7 %reduce-scatter.17.cloned.1.call-start = ((), (), s32[]{:S(2)}) async-start(), calls=%async_computation.13 | async-start | bytes 21897216 | tf_op jit(solution)/shard_map/reduce_scatter | solution.py:359
  1409.0 763.6 %reduce-scatter.13.cloned.1.call-start = ((), (), s32[]{:S(2)}) async-start(), calls=%async_computation.11 | async-start | bytes 21897216 | tf_op jit(solution)/shard_map/reduce_scatter | solution.py:395
  1422.6 975.5 %reduce-scatter.15.cloned.1.call-start = ((), (), s32[]{:S(2)}) async-start(), calls=%async_computation.12 | async-start | bytes 21897216 | tf_op jit(solution)/shard_map/reduce_scatter | solution.py:359
  1439.1 1344.5 %reduce-scatter.11.cloned.1.call-start = ((), (), s32[]{:S(2)}) async-start(), calls=%async_computation.10 | async-start | bytes 43794432 | tf_op jit(solution)/shard_map/reduce_scatter | solution.py:358
  1490.4 1677.2 %reduce-scatter.7.cloned.1.call-start = ((), (), s32[]{:S(2)}) async-start(), calls=%async_computation.8 | async-start | bytes 43794432 | tf_op jit(solution)/shard_map/reduce_scatter | solution.py:394
  1541.0 2012.1 %reduce-scatter.9.cloned.1.call-start = ((), (), s32[]{:S(2)}) async-start(), calls=%async_computation.9 | async-start | bytes 43794432 | tf_op jit(solution)/shard_map/reduce_scatter | solution.py:358
  1682.2 1873.4 %copy-start.87 = (f32[16128]{0:T(1024)}, f32[16128]{0:T(1024)S(1)}, u32[]{:S(2)}) copy-start(f32[16128]{0:T(1024)S(1)} %all-reduce.6) | copy-start | bytes 193540
  2398.1 1157.5 %copy-start.132 = (f32[3,288]{1,0:T(4,128)S(1)}, f32[3,288]{1,0:T(4,128)}, u32[]{:S(2)}) copy-start(f32[3,288]{1,0:T(4,128)} %get-tuple-element.126) | copy-start | bytes 10372
  2783.6 817.9 %copy-start.56 = (f32[288,1152]{1,0:T(8,128)S(1)}, f32[288,1152]{1,0:T(8,128)}, u32[]{:S(2)}) copy-start(f32[288,1152]{1,0:T(8,128)} %reduce-scatter.11.cloned.1.call-done) | copy-start | bytes 3981316
  (162 other events, 2187.6 us)
Sparse Core Ops, SparseCore 0:
  20.4 203.5 all-reduce.11
  227.5 339.9 all-gather.4
  571.0 184.8 all-gather.6
  973.0 116.6 all-reduce.13
  1395.3 324.4 all-reduce.15
  1726.1 219.7 reduce-scatter.16
  1953.4 219.1 reduce-scatter.12
  2179.0 219.0 reduce-scatter.14
  2405.7 377.8 reduce-scatter.10
  2789.9 377.6 reduce-scatter.6
  3175.1 377.9 reduce-scatter.8
where the time goes:
time: 3740 us; the launch traced here: 3720 us
  waiting for transfers between devices  2570 us (69%)
  matrix products  372 us (10%)
  local copies, waits for them, and re-layouts  300 us (8%)
  other arithmetic  247 us (7%)
  blocking collectives  205 us (5%)
    reduce_scatter x2, waiting for transfers between devices, local(): lax.psum_scatter(grad_rows_full, ('dp', 'fsdp'), scatter_dimension=0, til...  769 us
    reduce_scatter x2, waiting for transfers between devices, local(): lax.psum_scatter(grad_fc2_full, ('dp', 'fsdp'), scatter_dimension=0, tile...  449 us
    reduce_scatter x1, waiting for transfers between devices, local(): lax.psum_scatter(first_rows_full, ('dp', 'fsdp'), scatter_dimension=0, ti...  384 us
    all_gather x1, waiting for transfers between devices, local(): lax.all_gather(rows_w.astype(jnp.bfloat16), ('dp', 'fsdp'), axis=1, tiled...  307 us
    unnamed x14, waiting for transfers between devices  285 us
    reduce_scatter x1, waiting for transfers between devices, local(): lax.psum_scatter(first_fc2_full, ('dp', 'fsdp'), scatter_dimension=0, til...  227 us
    unnamed x377, local copies, waits for them, and re-layouts  173 us
    all_gather x1, waiting for transfers between devices, local(): lax.all_gather(fc2_w.astype(jnp.bfloat16), ('dp', 'fsdp'), axis=1, tiled=...  150 us
  transfers between devices with their start and end apart: 11, of which 11 were waited for; matrix products, arithmetic and copies ran while one was open for 9% of the time, Pallas kernels for 0%

commit v1 on v0

--- a/solution.py
+++ b/solution.py
@@ -1,8 +1,11 @@
+import functools
 import math
 
 import jax
 import jax.numpy as jnp
 from jax import lax
+from jax.experimental import pallas as pl
+from jax.experimental.pallas import tpu as pltpu
 from jax.sharding import PartitionSpec as P
 
 D = 1152
@@ -223,7 +226,7 @@
     )
 
 
-def local(
+def plain_local(
     latents,
     noise,
     lengths,
@@ -457,7 +460,918 @@
     )
 
 
+AXES = ("dp", "fsdp")
+MESH = pl.DeviceIdType.MESH
+LATE = 14
+MISC_ROWS = 144
+MISC_LATE = PIN + 1 + PIN + L
+SKIP_ROW = MISC_LATE + CLS
+ALIGN_ROW = SKIP_ROW + 2 * D
+
+
+def tree_fits(mesh):
+    layers, inner = mesh.shape["dp"], mesh.shape["fsdp"]
+    devices = layers * inner
+    rows = 8 * D // devices
+    return inner == 8 and layers == 4 and rows % 16 == 0 and (4 * D) % (inner * rows) == 0
+
+
+def swap(value, bit):
+    count = lax.axis_size(AXES)
+    return lax.ppermute(value, AXES, [(i, i ^ bit) for i in range(count)])
+
+
+def shift_layers(value, step, targets=None):
+    layers, inner = lax.axis_size("dp"), lax.axis_size("fsdp")
+    pairs = []
+    for i in range(layers * inner):
+        layer = (i // inner + step) % layers
+        if targets is None or layer in targets:
+            pairs.append((i, layer * inner + i % inner))
+    return lax.ppermute(value, AXES, pairs)
+
+
+def butterfly_sum(value):
+    bit = 1
+    while bit < lax.axis_size(AXES):
+        value = value + swap(value, bit)
+        bit *= 2
+    return value
+
+
+def small_gather(value):
+    rank = lax.axis_index(AXES)
+    held = value[None]
+    bit = 1
+    while bit < lax.axis_size(AXES):
+        other = swap(held, bit)
+        low = (rank // bit) % 2 == 0
+        held = jnp.where(
+            low, jnp.concatenate([held, other], axis=0), jnp.concatenate([other, held], axis=0)
+        )
+        bit *= 2
+    return held
+
+
+def gather_kernel(units, n_in, *refs):
+    ins = refs[:n_in]
+    outs = refs[n_in:2*n_in]
+    own, own_sem, store_sem, send_sem, recv_sem = refs[2*n_in:]
+    layers = lax.axis_size("dp")
+    z, inner = lax.axis_index("dp"), lax.axis_index("fsdp")
+    c, x, y = lax.rem(inner, 2), lax.rem(inner // 2, 2), inner // 4
+    me = z * 8 + inner
+    cross = {"c": inner + 1 - 2 * c, "x": inner + 2 - 4 * x, "y": inner + 4 - 8 * y}
+
+    barrier = pltpu.get_barrier_semaphore()
+    for way in "cxy":
+        pl.semaphore_signal(barrier, inc=1, device_id=(z, cross[way]), device_id_type=MESH)
+    @pl.when(z > 0)
+    def _():
+        pl.semaphore_signal(barrier, inc=1, device_id=(z - 1, inner), device_id_type=MESH)
+    @pl.when(z < layers - 1)
+    def _():
+        pl.semaphore_signal(barrier, inc=1, device_id=(z + 1, inner), device_id_type=MESH)
+
+    def load(u):
+        i, lead, row, rows, _, _ = units[u]
+        return pltpu.make_async_copy(ins[i].at[lead, pl.ds(row, rows)], own.at[u, pl.ds(0, rows)], own_sem.at[u])
+    def slot(u, d):
+        i, lead, row, rows, _, _ = units[u]
+        return outs[i].at[lead, d, pl.ds(row, rows)]
+    def store(u):
+        rows = units[u][3]
+        return pltpu.make_async_copy(own.at[u, pl.ds(0, rows)], slot(u, me), store_sem.at[u])
+    for u in range(len(units)): load(u).start()
+    pl.semaphore_wait(barrier, 3 + (z > 0).astype(jnp.int32) + (z < layers - 1).astype(jnp.int32))
+
+    sends = []
+    counts = [0] * len(units)
+    def remote(u, d, target, number, from_own=False):
+        rows = units[u][3]
+        src = own.at[u, pl.ds(0, rows)] if from_own else slot(u, d)
+        return pltpu.make_async_remote_copy(src_ref=src, dst_ref=slot(u, d), send_sem=send_sem.at[u, number], recv_sem=recv_sem.at[u, d], device_id=target, device_id_type=MESH)
+    def send(u, d, target, cond=None, from_own=False):
+        n = counts[u]; counts[u] += 1
+        sends.append((u, d, target, n, cond, from_own))
+        if cond is None: remote(u, d, target, n, from_own).start()
+        else:
+            @pl.when(cond)
+            def _(): remote(u, d, target, n, from_own).start()
+    def arrive(u, d, cond=None):
+        if cond is None: remote(u, d, (z, cross["c"]), 0).wait_recv()
+        else:
+            @pl.when(cond)
+            def _(): remote(u, d, (z, cross["c"]), 0).wait_recv()
+    up, down = (z + 1, inner), (z - 1, inner)
+    def side(way): return (z, cross[way])
+
+    def z_first(u):
+        first, second = units[u][5]
+        steps = []
+        def begin():
+            load(u).wait(); store(u).start()
+            send(u, me, up, z < layers - 1, True)
+            send(u, me, down, z > 0, True)
+            for w in (first, second): send(u, me, side(w), None, True)
+            send(u, me, side("c"), None, True)
+        steps.append(begin)
+        def from_z(k, below):
+            d = me - 8 * k if below else me + 8 * k
+            ok = (z >= k) if below else (z < layers - k)
+            def f():
+                arrive(u, d, ok)
+                if below: send(u, d, up, ok & (z < layers - 1))
+                else: send(u, d, down, ok & (z > 0))
+                for w in (first, second): send(u, d, side(w), ok)
+                send(u, d, side("c"), ok)
+            return f
+        for k in range(1, layers):
+            steps.append(from_z(k, True)); steps.append(from_z(k, False))
+        def from_side(k, below):
+            dz = 0 if k == 0 else (-8 * k if below else 8 * k)
+            ok = None if k == 0 else ((z >= k) if below else (z < layers - k))
+            def f():
+                d = z * 8 + dz + cross[first]
+                arrive(u, d, ok)
+                send(u, d, side(second), ok)
+                send(u, d, side("c"), ok)
+                d2 = z * 8 + dz + cross[second]
+                arrive(u, d2, ok)
+                send(u, d2, side("c"), ok)
+            return f
+        def from_far(k, below):
+            dz = 0 if k == 0 else (-8 * k if below else 8 * k)
+            ok = None if k == 0 else ((z >= k) if below else (z < layers - k))
+            def f():
+                d = z * 8 + dz + cross["x"] + cross["y"] - inner
+                arrive(u, d, ok)
+                send(u, d, side("c"), ok)
+            return f
+        order = [(0, True)] + [(k, b) for k in range(1, layers) for b in (True, False)]
+        for kb in order: steps.append(from_side(*kb))
+        for kb in order: steps.append(from_far(*kb))
+        return steps
+    def z_last(u):
+        first, second = units[u][5]
+        steps = []
+        def begin():
+            load(u).wait(); store(u).start()
+            for w in (first, second): send(u, me, side(w), None, True)
+            send(u, me, up, z < layers - 1, True)
+            send(u, me, down, z > 0, True)
+            send(u, me, side("c"), None, True)
+        steps.append(begin)
+        far = cross["x"] + cross["y"] - inner
+        def spread(d):
+            send(u, d, up, z < layers - 1)
+            send(u, d, down, z > 0)
+            send(u, d, side("c"))
+        def f1():
+            d = z * 8 + cross[first]; arrive(u, d); send(u, d, side(second)); spread(d)
+            d = z * 8 + cross[second]; arrive(u, d); spread(d)
+        def f2():
+            d = z * 8 + far; arrive(u, d); spread(d)
+        steps += [f1, f2]
+        def from_z(k, below):
+            ok = (z >= k) if below else (z < layers - k)
+            def f():
+                for col in (inner, cross[first], cross[second], far):
+                    d = (z - k if below else z + k) * 8 + col
+                    arrive(u, d, ok)
+                    if below: send(u, d, up, ok & (z < layers - 1))
+                    else: send(u, d, down, ok & (z > 0))
+                    send(u, d, side("c"), ok)
+            return f
+        for k in range(1, layers):
+            steps.append(from_z(k, True)); steps.append(from_z(k, False))
+        return steps
+    plans = [z_first(u) if units[u][4] == "z" else z_last(u) for u in range(len(units))]
+    agenda = sorted(
+        ((s if units[u][4] == "z" or s < 3 else LATE + s - 3) + u, u, s)
+        for u in range(len(units))
+        for s in range(len(plans[u]))
+    )
+    for _, u, s in agenda: plans[u][s]()
+    for u in range(len(units)):
+        for d in range(layers * 4):
+            arrive(u, 2 * d + 1 - c)
+        store(u).wait()
+    for u, d, target, n, cond, from_own in sends:
+        if cond is None: remote(u, d, target, n, from_own).wait_send()
+        else:
+            @pl.when(cond)
+            def _(u=u, d=d, target=target, n=n, from_own=from_own): remote(u, d, target, n, from_own).wait_send()
+
+def gather_all(units, arrays, cid=0):
+    devices = lax.axis_size(("dp","fsdp"))
+    U = len(units)
+    rows = max(u[3] for u in units)
+    width = arrays[0].shape[-1]
+    return pl.pallas_call(
+        functools.partial(gather_kernel, units, len(arrays)),
+        out_shape=[jax.ShapeDtypeStruct((a.shape[0], devices) + a.shape[1:], a.dtype) for a in arrays],
+        in_specs=[pl.BlockSpec(memory_space=pl.ANY)] * len(arrays),
+        out_specs=[pl.BlockSpec(memory_space=pl.ANY)] * len(arrays),
+        scratch_shapes=[pltpu.VMEM((U, rows, width), jnp.bfloat16), pltpu.SemaphoreType.DMA((U,)), pltpu.SemaphoreType.DMA((U,)),
+            pltpu.SemaphoreType.DMA((U, 64)), pltpu.SemaphoreType.DMA((U, devices))],
+        compiler_params=pltpu.CompilerParams(collective_id=cid, has_side_effects=True, vmem_limit_bytes=16<<20),
+        name="gather_all")(*arrays)
+
+
+def gather_weights(rows, fc2, misc):
+    rows_each, half = rows.shape[1], rows.shape[1] // 2
+    ways = (("x", "y"), ("y", "x"))
+    units = [(2, 0, 0, misc.shape[1], "last", ways[0]), (1, 0, 0, fc2.shape[1], "last", ways[1])]
+    for block_id in range(BLOCKS):
+        units += [(0, block_id, row, half, "z", ways[row // half]) for row in (0, half)]
+        if block_id > 0:
+            units.append((1, block_id, 0, fc2.shape[1], "z", ways[block_id % 2]))
+    return gather_all(units, [rows, fc2, misc])
+
+
+def greet(partners):
+    barrier = pltpu.get_barrier_semaphore()
+    for partner in partners:
+        pl.semaphore_signal(barrier, inc=1, device_id=partner, device_id_type=MESH)
+    pl.semaphore_wait(barrier, len(partners))
+
+
+def owner_sum_kernel(groups, *refs):
+    n = len(groups)
+    ys, xs = refs[:n], refs[n : 2 * n]
+    outs = refs[2 * n : 3 * n]
+    scratch = refs[3 * n :]
+    names = ("y_own", "y_far", "x_far", "part", "got_one", "got_two", "got_z",
+             "load_sem", "ex_send", "ex_recv", "x_sem", "part_send", "one_recv", "two_recv", "z_send", "z_recv")
+    per = len(names)
+    layers = lax.axis_size("dp")
+    z, inner = lax.axis_index("dp"), lax.axis_index("fsdp")
+    c, x, y = lax.rem(inner, 2), lax.rem(inner // 2, 2), inner // 4
+    other = (z, inner + 1 - 2 * c)
+    sides = ((z, inner + 2 - 4 * x), (z, inner + 4 - 8 * y))
+    columns = [(lax.rem(z + k, layers), inner) for k in range(1, layers)]
+
+    def chip_of(group, slot):
+        b, a = lax.rem(slot // 2, 2), lax.rem(slot, 2)
+        yy, xx = y + b - 2 * y * b, x + a - 2 * x * a
+        return (slot // 4) * 4 + yy * 2 + xx
+
+    parts = []
+    for g, group in enumerate(groups):
+        s = dict(zip(names, scratch[g * per : (g + 1) * per]))
+        s.update(y=ys[g], x=xs[g], x_own=xs[g], out=outs[g], group=group, slots=4 * group[1])
+        parts.append(s)
+
+    def x_there(s):
+        return pltpu.make_async_remote_copy(
+            src_ref=s["x"], dst_ref=s["x_far"], send_sem=s["x_sem"].at[0], recv_sem=s["x_sem"].at[1],
+            device_id=other, device_id_type=MESH)
+
+    def y_here(s, slot):
+        return pltpu.make_async_copy(s["y"].at[chip_of(s["group"], slot), c], s["y_own"].at[slot], s["load_sem"].at[slot])
+
+    def y_there(s, slot):
+        return pltpu.make_async_remote_copy(
+            src_ref=s["y"].at[chip_of(s["group"], slot), 1 - c], dst_ref=s["y_far"].at[slot],
+            send_sem=s["ex_send"].at[slot], recv_sem=s["ex_recv"].at[slot], device_id=other, device_id_type=MESH)
+
+    def slot_of(kind, layer, first, second):
+        return layer * 4 + (second * 2 + first if kind == 0 else first * 2 + second)
+
+    def one_there(s, kind, layer, second):
+        return pltpu.make_async_remote_copy(
+            src_ref=s["part"].at[slot_of(kind, layer, 1, second)], dst_ref=s["got_one"].at[layer * 2 + second],
+            send_sem=s["part_send"].at[slot_of(kind, layer, 1, second)], recv_sem=s["one_recv"].at[layer * 2 + second],
+            device_id=sides[kind], device_id_type=MESH)
+
+    def two_there(s, kind, layer):
+        return pltpu.make_async_remote_copy(
+            src_ref=s["part"].at[slot_of(kind, layer, 0, 1)], dst_ref=s["got_two"].at[layer],
+            send_sem=s["part_send"].at[slot_of(kind, layer, 0, 1)], recv_sem=s["two_recv"].at[layer],
+            device_id=sides[1 - kind], device_id_type=MESH)
+
+    def z_there(s, kind, layer):
+        target = s["group"][0] + layer
+        hop = lax.rem(target - z + layers, layers)
+        spot = jnp.maximum(hop - 1, 0)
+        return pltpu.make_async_remote_copy(
+            src_ref=s["part"].at[slot_of(kind, layer, 0, 0)], dst_ref=s["got_z"].at[spot],
+            send_sem=s["z_send"].at[layer], recv_sem=s["z_recv"].at[spot],
+            device_id=(target, inner), device_id_type=MESH)
+
+    def product(s, slot):
+        y_here(s, slot).wait()
+        y_there(s, slot).wait_recv()
+        if s["group"][2] > 1:
+            rows = s["out"].shape[0]
+            owner = (s["group"][0] * 4 + chip_of(s["group"], slot)) * 2 + c
+            kind = (owner * rows >= s["group"][3]).astype(jnp.int32)
+        else:
+            kind = 0
+        return jnp.dot(s["y_own"][slot], s["x_own"][kind], preferred_element_type=jnp.float32) + jnp.dot(
+            s["y_far"][slot], s["x_far"][kind], preferred_element_type=jnp.float32)
+
+    greet([other, *sides, *columns])
+    for s in parts:
+        x_there(s).start()
+        @pl.loop(0, s["slots"])
+        def _(i):
+            y_there(s, i).start()
+    for s in parts:
+        half = (s["group"][1] + 1) // 2
+        s["kinds"] = [(0, 0, half), (1, half, s["group"][1])]
+    def first_step(s):
+        x_there(s).wait_recv()
+        for kind, lo, hi in s["kinds"]:
+            for second in (1, 0):
+                @pl.loop(lo, hi)
+                def _(layer):
+                    slot = slot_of(kind, layer, 1, second)
+                    s["part"][slot] = product(s, slot).astype(jnp.bfloat16)
+                    one_there(s, kind, layer, second).start()
+    def second_step(s):
+        for kind, lo, hi in s["kinds"]:
+            @pl.loop(lo, hi)
+            def _(layer):
+                slot = slot_of(kind, layer, 0, 1)
+                own = product(s, slot)
+                one_there(s, kind, layer, 1).wait_recv()
+                s["part"][slot] = (own + s["got_one"][layer * 2 + 1].astype(jnp.float32)).astype(jnp.bfloat16)
+                two_there(s, kind, layer).start()
+    def third_step(s):
+        for kind, lo, hi in s["kinds"]:
+            @pl.loop(lo, hi)
+            def _(layer):
+                slot = slot_of(kind, layer, 0, 0)
+                own = product(s, slot)
+                one_there(s, kind, layer, 0).wait_recv()
+                two_there(s, kind, layer).wait_recv()
+                total = own + s["got_one"][layer * 2].astype(jnp.float32) + s["got_two"][layer].astype(jnp.float32)
+                s["part"][slot] = total.astype(jnp.bfloat16)
+                @pl.when(s["group"][0] + layer != z)
+                def _():
+                    z_there(s, kind, layer).start()
+    def last_step(s):
+        lo, count = s["group"][:2]
+        inside = (z >= lo) & (z < lo + count)
+        for kind, a, b in s["kinds"]:
+            @pl.loop(a, b)
+            def _(layer):
+                @pl.when(lo + layer == z)
+                def _():
+                    total = s["part"][slot_of(kind, layer, 0, 0)].astype(jnp.float32)
+                    for k in range(layers - 1):
+                        pltpu.make_async_remote_copy(
+                            src_ref=s["got_z"].at[k], dst_ref=s["got_z"].at[k], send_sem=s["z_send"].at[0],
+                            recv_sem=s["z_recv"].at[k], device_id=columns[0], device_id_type=MESH).wait_recv()
+                        total = total + s["got_z"][k].astype(jnp.float32)
+                    s["out"][...] = total
+        if count < layers:
+            @pl.when(jnp.logical_not(inside))
+            def _():
+                s["out"][...] = jnp.zeros_like(s["out"])
+    for s in parts:
+        @pl.loop(0, s["slots"])
+        def _(i):
+            y_here(s, i).start()
+    for s in parts:
+        first_step(s)
+    for s in parts:
+        second_step(s)
+    for s in parts:
+        third_step(s)
+    for s in parts:
+        last_step(s)
+    for s in parts:
+        x_there(s).wait_send()
+        @pl.loop(0, s["slots"])
+        def _(i):
+            y_there(s, i).wait_send()
+        for kind, lo, hi in s["kinds"]:
+            @pl.loop(lo, hi)
+            def _(layer):
+                for second in (0, 1):
+                    one_there(s, kind, layer, second).wait_send()
+                two_there(s, kind, layer).wait_send()
+                @pl.when(s["group"][0] + layer != z)
+                def _():
+                    z_there(s, kind, layer).wait_send()
+
+
+def owner_sums(groups, ys, xs, cid):
+    scratch = []
+    shapes = []
+    layers = lax.axis_size("dp")
+    for group, y, x in zip(groups, ys, xs):
+        count, (rows, tokens) = group[1], y.shape[2:]
+        slots = 4 * count
+        dma = pltpu.SemaphoreType.DMA
+        low = jnp.bfloat16
+        scratch += [
+            pltpu.VMEM((slots, rows, tokens), low),
+            pltpu.VMEM((slots, rows, tokens), low),
+            pltpu.VMEM(x.shape, low),
+            pltpu.VMEM((slots, rows, D), low),
+            pltpu.VMEM((2 * count, rows, D), low),
+            pltpu.VMEM((count, rows, D), low),
+            pltpu.VMEM((layers - 1, rows, D), low),
+            dma((slots,)), dma((slots,)), dma((slots,)), dma((2,)), dma((slots,)), dma((2 * count,)), dma((count,)), dma((count,)), dma((layers - 1,)),
+        ]
+        shapes.append(jax.ShapeDtypeStruct((rows, D), jnp.float32))
+    return pl.pallas_call(
+        functools.partial(owner_sum_kernel, groups),
+        out_shape=shapes,
+        in_specs=[pl.BlockSpec(memory_space=pl.ANY)] * len(ys) + [pl.BlockSpec(memory_space=pltpu.VMEM)] * len(xs),
+        out_specs=[pl.BlockSpec(memory_space=pltpu.VMEM)] * len(ys),
+        scratch_shapes=scratch,
+        compiler_params=pltpu.CompilerParams(collective_id=cid, has_side_effects=True, vmem_limit_bytes=60 << 20),
+        name="owner_sums",
+    )(*ys, *xs)
+
+
+def product_kernel(table, y_own, y_other, x_own, x_other, out):
+    out[0] = (
+        jnp.dot(y_own[0], x_own[0], preferred_element_type=jnp.float32)
+        + jnp.dot(y_other[0], x_other[0], preferred_element_type=jnp.float32)
+    ).astype(jnp.bfloat16)
+
+
+def products(table, count, y_own, y_other, x_own, x_other):
+    rows, tokens = y_own.shape[1:]
+    width = x_own.shape[-1]
+    return pl.pallas_call(
+        product_kernel,
+        out_shape=jax.ShapeDtypeStruct((count, rows, width), jnp.bfloat16),
+        grid_spec=pltpu.PrefetchScalarGridSpec(
+            num_scalar_prefetch=1,
+            grid=(count,),
+            in_specs=[
+                pl.BlockSpec((1, rows, tokens), lambda n, t: (t[n], 0, 0)),
+                pl.BlockSpec((1, rows, tokens), lambda n, t: (t[count + n], 0, 0)),
+                pl.BlockSpec((1, tokens, width), lambda n, t: (t[2 * count + n], 0, 0)),
+                pl.BlockSpec((1, tokens, width), lambda n, t: (t[2 * count + n], 0, 0)),
+            ],
+            out_specs=pl.BlockSpec((1, rows, width), lambda n, t: (n, 0, 0)),
+        ),
+        compiler_params=pltpu.CompilerParams(vmem_limit_bytes=24 << 20),
+        cost_estimate=pl.CostEstimate(
+            flops=4 * count * rows * tokens * width,
+            bytes_accessed=2 * count * rows * (width + 2 * tokens),
+            transcendentals=0,
+        ),
+        name="products",
+    )(table, y_own, y_other, x_own, x_other)
+
+
+def add_low(*terms):
+    total = terms[0].astype(jnp.float32)
+    for term in terms[1:]:
+        total = total + term.astype(jnp.float32)
+    return total.astype(jnp.bfloat16)
+
+
+def scatter_products(y_parts, x_parts, layers_here, kind_of):
+    inner = lax.axis_index("fsdp")
+    core, x_bit, y_bit = inner % 2, (inner // 2) % 2, inner // 4
+    count_layers = len(layers_here)
+    rows, tokens = y_parts.shape[1:]
+    by_core = y_parts.reshape(count_layers * 4, 2, rows, tokens)
+    sent = lax.dynamic_index_in_dim(by_core, 1 - core, axis=1, keepdims=False)
+    y_other = swap(sent, 1)
+    x_other = swap(x_parts, 1)
+    half = (count_layers + 1) // 2
+
+    def table_of(spots):
+        own, other, kinds = [], [], []
+        for place, flip_x, flip_y in spots:
+            chip = place * 4 + (y_bit ^ flip_y) * 2 + (x_bit ^ flip_x)
+            own.append(2 * chip + core)
+            other.append(chip)
+            kinds.append(kind_of(layers_here[0] * 8 + 2 * chip + core))
+        return jnp.stack(own + other + kinds).astype(jnp.int32)
+
+    def make(spots, lead):
+        made = products(table_of(spots), len(spots), y_parts, y_other, x_parts, x_other)
+        return made.reshape(lead + (rows, D))
+
+    halves = []
+    for which, places in enumerate((range(half), range(half, count_layers))):
+        if len(places) == 0:
+            continue
+        n = len(places)
+        first, second = ((2, 4), (4, 2))[which]
+        spots = {}
+        for flip_first in (1, 0):
+            spots[flip_first] = [
+                (p, flip_first, flip_second) if which == 0 else (p, flip_second, flip_first)
+                for flip_second in (0, 1)
+                for p in places
+            ]
+        away = swap(make(spots[1], (2, n)), first)
+        kept = make(spots[0], (2, n))
+        far = swap(add_low(kept[1], away[1]), second)
+        halves.append(add_low(kept[0], away[0], far))
+    summed = halves[0] if len(halves) == 1 else jnp.concatenate(halves, axis=0)
+    return scatter_layers(summed, layers_here)
+
+
+def scatter_layers(summed, layers_here):
+    layer = lax.axis_index("dp")
+    layers = lax.axis_size("dp")
+
+    def for_layer(target):
+        spot = jnp.clip(target - layers_here[0], 0, len(layers_here) - 1)
+        return lax.dynamic_index_in_dim(summed, spot, axis=0, keepdims=False)
+
+    total = for_layer(layer).astype(jnp.float32)
+    for k in range(1, layers):
+        got = shift_layers(for_layer((layer + k) % layers), k, layers_here)
+        total = total + got.astype(jnp.float32)
+    return total
+
+
+def scatter_first_layer(full):
+    inner = lax.axis_index("fsdp")
+    held = full.astype(jnp.bfloat16).reshape(2, 2, 2, full.shape[1], D)
+    for axis, bit in ((2, 1), (1, 2), (0, 4)):
+        mine = (inner // bit) % 2
+        away = swap(lax.dynamic_index_in_dim(held, 1 - mine, axis=axis, keepdims=False), bit)
+        kept = lax.dynamic_index_in_dim(held, mine, axis=axis, keepdims=False)
+        held = add_low(kept, away)
+    return scatter_layers(held[None], [0])
+
+
+def dot(left, right, over, batch=((), ())):
+    return lax.dot_general(
+        left, right, ((over[:1], over[1:]), batch), preferred_element_type=jnp.float32
+    )
+
+
+HEADS = ((0,), (0,))
+
+
+def masked_scores(queries, keys_all, keymask):
+    scores = dot(queries, keys_all, (1, 1), HEADS) * HD ** (-0.5)
+    return jnp.where(keymask[None, None, :], scores, mask_fill)
+
+
+def fast_forward(hidden, weights, fc2, gvec, keymask):
+    normed, save_one = layer_norm(hidden, gvec[0], gvec[1])
+    normed_low = normed.astype(jnp.bfloat16)
+    triple = dot(weights[: 3 * D], normed_low, (1, 1)).astype(jnp.bfloat16).reshape(3, H, HD, L)
+    scores = masked_scores(triple[0], triple[1], keymask)
+    highest = jnp.max(scores, axis=-1, keepdims=True)
+    logsum = highest + jnp.log(jnp.sum(jnp.exp(scores - highest), axis=-1, keepdims=True))
+    probs = jnp.exp(scores - logsum).astype(jnp.bfloat16)
+    attended = dot(triple[2], probs, (2, 2), HEADS).astype(jnp.bfloat16).reshape(D, L)
+    after = hidden + dot(attended, weights[3 * D : 4 * D], (0, 1))
+    normed_two, save_two = layer_norm(after, gvec[2], gvec[3])
+    normed_two_low = normed_two.astype(jnp.bfloat16)
+    inner = dot(weights[4 * D :], normed_two_low, (1, 1))
+    active = jax.nn.gelu(inner, approximate=True).astype(jnp.bfloat16)
+    output = after + dot(active, fc2, (0, 0))
+    return output, (
+        save_one,
+        normed_low,
+        triple,
+        logsum,
+        attended,
+        save_two,
+        normed_two_low,
+        inner,
+        active,
+    )
+
+
+def fast_backward(dout, weights, fc2, gvec, keymask, saved):
+    save_one, normed_low, triple, logsum, attended, save_two, normed_two_low, inner, active = saved
+    devices = lax.axis_size(AXES)
+    layers = lax.axis_size("dp")
+    rows_each = 8 * D // devices
+    dlow = dout.astype(jnp.bfloat16)
+    dactive = dot(fc2, dlow, (1, 1))
+    slope = jax.vjp(lambda entry: jax.nn.gelu(entry, approximate=True), inner)[1](dactive)[0]
+    dinner = slope.astype(jnp.bfloat16)
+    dnormed_two = dot(dinner, weights[4 * D :], (0, 0))
+    dafter_norm, dgain_two, dbias_two = norm_back(dnormed_two, save_two, gvec[2])
+    dafter = dout + dafter_norm
+    dafter_low = dafter.astype(jnp.bfloat16)
+    dattended = dot(weights[3 * D : 4 * D], dafter_low, (0, 1)).astype(jnp.bfloat16)
+    dattended = dattended.reshape(H, HD, L)
+    probs = jnp.exp(masked_scores(triple[0], triple[1], keymask) - logsum)
+    dprobs = dot(dattended, triple[2], (1, 1), HEADS)
+    dscores = (probs * (dprobs - jnp.sum(probs * dprobs, axis=-1, keepdims=True))).astype(
+        jnp.bfloat16
+    )
+    dqueries = dot(triple[1], dscores, (2, 2), HEADS) * HD ** (-0.5)
+    dkeys = dot(triple[0], dscores, (2, 1), HEADS) * HD ** (-0.5)
+    dvalues = dot(dattended, probs.astype(jnp.bfloat16), (2, 1), HEADS)
+    dtriple = jnp.stack([dqueries, dkeys, dvalues]).astype(jnp.bfloat16).reshape(3 * D, L)
+    lower_parts = jnp.concatenate([dtriple, dafter_low.T], axis=0)
+    half = layers // 2
+    groups = [(0, layers, 1, 0), (half, layers - half, 1, 0), (0, half, 2, 3 * D)]
+    grad_fc2, grad_upper, grad_lower = owner_sums(
+        groups,
+        [
+            active.reshape(devices // 2, 2, rows_each // 2, L),
+            dinner.reshape(devices // 4, 2, rows_each, L),
+            lower_parts.reshape(devices // 4, 2, rows_each, L),
+        ],
+        [dlow[None], normed_two_low[None], jnp.stack([normed_low, attended.T])],
+        1,
+    )
+    dnormed = dot(dtriple, weights[: 3 * D], (0, 0))
+    dhidden_norm, dgain_one, dbias_one = norm_back(dnormed, save_one, gvec[0])
+    gain_grad = jnp.stack([dgain_one, dbias_one, dgain_two, dbias_two])
+    grad_rows = jnp.where(lax.axis_index("dp") >= half, grad_upper, grad_lower)
+    return dafter + dhidden_norm, grad_rows, grad_fc2, gain_grad
+
+
+def row_starts(devices, misc_here):
+    return [(d * misc_here) // D for d in range(devices)]
+
+
+def misc_rows(pieces, starts, lo, hi):
+    total = jnp.zeros((hi - lo, D), pieces.dtype)
+    used = MISC_ROWS - 4
+    for d, start in enumerate(starts):
+        first, last = max(start, lo), min(start + used, hi)
+        if first < last:
+            part = pieces[d, first - start : last - start]
+            total = total + jnp.pad(part, ((first - lo, hi - last), (0, 0)))
+    return total
+
+
+def fast_local(
+    latents,
+    noise,
+    lengths,
+    timesteps,
+    labels,
+    enc_feats,
+    pair_idx,
+    step,
+    rows_w,
+    fc2_w,
+    misc_w,
+    gains,
+    rows_m,
+    rows_v,
+    fc2_m,
+    fc2_v,
+    misc_m,
+    misc_v,
+    gains_m,
+    gains_v,
+):
+    rank_here = lax.axis_index(AXES)
+    total_items = devices = lax.axis_size(AXES)
+    layers = lax.axis_size("dp")
+    misc_here, gains_here = misc_w.shape[0], gains.shape[0]
+    starts = row_starts(devices, misc_here)
+    start_here = (rank_here * misc_here) // D
+    offset_here = rank_here * misc_here - start_here * D
+
+    encoded = (
+        enc_feats * lax.rsqrt(jnp.sum(enc_feats * enc_feats, axis=-1, keepdims=True) + vector_eps)
+    ).astype(jnp.bfloat16)
+    used = MISC_ROWS - 4
+    flat = lax.dynamic_update_slice(
+        jnp.zeros((used * D,), jnp.bfloat16), misc_w.astype(jnp.bfloat16), (offset_here,)
+    )
+    extra = jnp.stack(
+        [
+            jnp.pad(gains.astype(jnp.bfloat16), (0, D - gains_here)),
+            jnp.pad(encoded[0], (0, D - ENC)),
+            jnp.pad(pair_idx.astype(jnp.bfloat16), (0, D - 1)),
+            jnp.zeros((D,), jnp.bfloat16),
+        ]
+    )
+    piece_misc = jnp.concatenate([flat.reshape(used, D), extra], axis=0)
+    rows_full, fc2_full, misc_full = gather_weights(
+        rows_w.astype(jnp.bfloat16), fc2_w.astype(jnp.bfloat16), piece_misc[None]
+    )
+    pieces = misc_full[0]
+    rows_all = [rows_full[block_id].reshape(8 * D, D) for block_id in range(BLOCKS)]
+    fc2_all = [fc2_full[block_id].reshape(4 * D, D) for block_id in range(BLOCKS)]
+
+    gains_all = pieces[:, used, :gains_here].reshape(-1)
+    gain_rows = gains_all.astype(jnp.float32).reshape(-1, D)
+    encoded_all = pieces[:, used + 1, :ENC]
+    pairs_all = pieces[:, used + 2, 0].astype(jnp.int32)
+    front = misc_rows(pieces, starts, 0, MISC_LATE)
+    embed = front[: PIN + 1]
+    head = front[PIN + 1 : 2 * PIN + 1].reshape(D, PIN)
+    posit = front[2 * PIN + 1 :].astype(jnp.float32)
+    skip = misc_rows(pieces, starts, SKIP_ROW, ALIGN_ROW)
+    align = misc_rows(pieces, starts, ALIGN_ROW, ALIGN_ROW + ENC).reshape(D, ENC)
+    class_place = MISC_LATE + labels[0]
+    owner_first = (class_place * D) // misc_here
+    owner_last = (class_place * D + D - 1) // misc_here
+
+    def class_part(owner):
+        return lax.dynamic_slice(
+            pieces, (owner, class_place - (owner * misc_here) // D, 0), (1, 1, D)
+        )[0].astype(jnp.float32)
+
+    class_row = class_part(owner_first) + jnp.where(
+        owner_last > owner_first, class_part(owner_last), 0.0
+    )
+
+    keymask = jnp.arange(L) < lengths[0] + 2
+    valid = (jnp.arange(PATCH) < lengths[0]).astype(jnp.float32)[:, None]
+    live_count = lengths[0].astype(jnp.float32)
+    patches = jnp.dot(latents[0], embed[:PIN], preferred_element_type=jnp.float32) + embed[
+        PIN
+    ].astype(jnp.float32)
+    tokens = jnp.concatenate([time_embed(timesteps), class_row, patches], axis=0) + posit
+
+    def gvec(block_id):
+        return gain_rows[4 * block_id : 4 * block_id + 4]
+
+    shallow, saved_shallow = fast_forward(tokens, rows_all[0], fc2_all[0], gvec(0), keymask)
+    middle, saved_middle = fast_forward(shallow, rows_all[1], fc2_all[1], gvec(1), keymask)
+    joined = jnp.concatenate([middle, shallow], axis=-1).astype(jnp.bfloat16)
+    deep_in = jnp.dot(joined, skip, preferred_element_type=jnp.float32)
+    deep, saved_deep = fast_forward(deep_in, rows_all[2], fc2_all[2], gvec(2), keymask)
+
+    pooled = (jnp.sum(middle[2:] * valid, axis=0) / live_count).astype(jnp.bfloat16)
+    pooled_all = small_gather(pooled)
+    projected = jnp.dot(pooled_all, align, preferred_element_type=jnp.float32)
+    inverse = lax.rsqrt(jnp.sum(projected * projected, axis=-1, keepdims=True) + vector_eps)
+    zhat = projected * inverse
+    logits = gram_crossing(encoded_all, zhat.astype(jnp.bfloat16)) / logit_softening_scale
+    highest = jnp.max(logits, axis=-1, keepdims=True)
+    logsum = highest + jnp.log(jnp.sum(jnp.exp(logits - highest), axis=-1, keepdims=True))
+    target = (jnp.arange(total_items)[None, :] == pairs_all[:, None]).astype(jnp.float32)
+    align_loss = jnp.sum(logsum[:, 0] - jnp.sum(target * logits, axis=-1)) / total_items
+    dlogits = ((jnp.exp(logits - logsum) - target) * (align_weight / total_items)).astype(
+        jnp.bfloat16
+    )
+    dzhat = collected_sample_embeddings(dlogits, encoded_all) / logit_softening_scale
+    dproj = (inverse * (dzhat - zhat * jnp.sum(dzhat * zhat, axis=-1, keepdims=True))).astype(
+        jnp.bfloat16
+    )
+    grad_align = collected_sample_embeddings(pooled_all, dproj).reshape(ENC, D)
+    dpooled = gram_crossing(lax.dynamic_slice_in_dim(dproj, rank_here, 1, axis=0), align)
+    dmid_extra = jnp.pad(valid * dpooled / live_count, ((2, 0), (0, 0)))
+
+    final, save_final = layer_norm(deep[2:], gain_rows[12], gain_rows[13])
+    final_low = final.astype(jnp.bfloat16)
+    pred = jnp.dot(final_low, head, preferred_element_type=jnp.float32)
+    denom = live_count * PIN
+    diff = (pred - noise[0]) * valid
+    mse_local = jnp.sum(diff * diff) / denom / total_items
+    dpred = (2.0 * diff / denom / total_items).astype(jnp.bfloat16)
+    grad_head = collected_sample_embeddings(final_low, dpred)
+    dfinal, dgain_final, dbias_final = norm_back(
+        gram_crossing(dpred, head), save_final, gain_rows[12]
+    )
+
+    rows_grads = [None] * BLOCKS
+    fc2_grads = [None] * BLOCKS
+    gain_grads = [None] * BLOCKS
+    dhidden = jnp.pad(dfinal, ((2, 0), (0, 0)))
+    dhidden, rows_grads[2], fc2_grads[2], gain_grads[2] = fast_backward(
+        dhidden, rows_all[2], fc2_all[2], gvec(2), keymask, saved_deep
+    )
+    dlow = dhidden.astype(jnp.bfloat16)
+    joined_features = joined.T
+    skip_parts = []
+    for d in range(devices // layers, devices):
+        first = max(starts[d], SKIP_ROW)
+        last = min(starts[d] + used, ALIGN_ROW)
+        if first < last:
+            part = joined_features[first - SKIP_ROW : last - SKIP_ROW]
+            part = jnp.pad(
+                part, ((first - starts[d], MISC_ROWS - (last - starts[d])), (0, 0))
+            )
+        else:
+            part = jnp.zeros((MISC_ROWS, L), jnp.bfloat16)
+        skip_parts.append(part)
+    grad_skip = scatter_products(
+        jnp.stack(skip_parts), dlow[None], list(range(1, layers)), lambda owner: owner * 0
+    )
+    djoined = gram_crossing(dlow, skip)
+    dhidden = djoined[:, :D] + dmid_extra
+    dshort = djoined[:, D:]
+    dhidden, rows_grads[1], fc2_grads[1], gain_grads[1] = fast_backward(
+        dhidden, rows_all[1], fc2_all[1], gvec(1), keymask, saved_middle
+    )
+    dhidden = dhidden + dshort
+    dhidden, rows_grads[0], fc2_grads[0], gain_grads[0] = fast_backward(
+        dhidden, rows_all[0], fc2_all[0], gvec(0), keymask, saved_shallow
+    )
+
+    dpatch = dhidden[2:]
+    grad_embed = collected_sample_embeddings(latents[0], dpatch.astype(jnp.bfloat16))
+    late = jnp.concatenate(
+        [
+            grad_embed,
+            jnp.sum(dpatch, axis=0, keepdims=True),
+            grad_head.reshape(PIN, D),
+            dhidden,
+        ],
+        axis=0,
+    )
+    inner = devices // layers
+    late_parts = []
+    for d in range(inner):
+        first, last = starts[d], min(starts[d] + used, MISC_LATE)
+        if first < last:
+            late_parts.append(jnp.pad(late[first:last], ((0, MISC_ROWS - (last - first)), (0, 0))))
+        else:
+            late_parts.append(jnp.zeros((MISC_ROWS, D), jnp.float32))
+    grad_late = scatter_first_layer(jnp.stack(late_parts))
+    class_grads = small_gather(dhidden[1])
+    class_rows = MISC_LATE + small_gather(labels.astype(jnp.float32)).astype(jnp.int32)[:, 0]
+    hit = (
+        class_rows[None, :] == start_here + jnp.arange(MISC_ROWS)[:, None]
+    ).astype(jnp.float32)
+    grad_class = jnp.dot(
+        hit, class_grads, precision=lax.Precision.HIGHEST, preferred_element_type=jnp.float32
+    )
+    align_first = starts[-1] + MISC_ROWS
+    grad_align = jnp.pad(
+        grad_align, ((MISC_ROWS, align_first - (ALIGN_ROW + ENC)), (0, 0))
+    )
+    align_here = lax.dynamic_slice_in_dim(
+        grad_align, jnp.maximum(start_here - (ALIGN_ROW - MISC_ROWS), 0), MISC_ROWS, axis=0
+    )
+    grad_piece = (
+        jnp.where(lax.axis_index("dp") == 0, grad_late, grad_skip) + grad_class + align_here
+    )
+    misc_shard = lax.dynamic_slice(grad_piece.reshape(-1), (offset_here,), (misc_here,))
+    gains_sum = butterfly_sum(
+        jnp.concatenate(
+            [
+                gain_grads[0],
+                gain_grads[1],
+                gain_grads[2],
+                jnp.stack([dgain_final, dbias_final]),
+                jnp.zeros((2, D), jnp.float32),
+            ],
+            axis=0,
+        )
+    )
+    gains_shard = lax.dynamic_slice_in_dim(
+        gains_sum.reshape(-1), rank_here * gains_here, gains_here
+    )
+
+    grads = (jnp.stack(rows_grads), jnp.stack(fc2_grads), misc_shard, gains_shard)
+    weights = (rows_w, fc2_w, misc_w, gains)
+    firsts = (rows_m, fc2_m, misc_m, gains_m)
+    seconds = (rows_v, fc2_v, misc_v, gains_v)
+    kinds = segment_kinds(rank_here, rows_w.shape[1], misc_w.shape[0])
+    matrices = 4 * BLOCKS + 7
+    sums = butterfly_sum(
+        jnp.concatenate(
+            [
+                squares(kinds, grads[0], grads[1], grads[2], grads[3]),
+                squares(kinds, rows_w, fc2_w, misc_w, gains),
+                mse_local[None],
+            ]
+        )
+    )
+    weight_squares = sums[matrices : 2 * matrices]
+    loss = sums[2 * matrices] + align_weight * align_loss
+    grad_norm = jnp.sqrt(jnp.sum(sums[:matrices]))
+    factor = jnp.minimum(1.0, clip_limit / grad_norm)
+    count = step[0].astype(jnp.float32)
+    moved = [
+        adam_move(
+            grads[member],
+            weights[member],
+            firsts[member],
+            seconds[member],
+            factor,
+            count,
+            weight_decay if member < 3 else 0.0,
+        )
+        for member in range(4)
+    ]
+    updates = [entry[2] for entry in moved]
+    update_squares = butterfly_sum(squares(kinds, updates[0], updates[1], updates[2], updates[3]))
+    ratios = jnp.sqrt(weight_squares) / jnp.sqrt(update_squares + vector_eps)
+    ratio_maps = spread(ratios, kinds, BLOCKS)
+    renewed = [
+        weights[member] - learn_rate * ratio_maps[member] * updates[member] for member in range(4)
+    ]
+    norms = jnp.stack([jnp.sqrt(weight_squares), jnp.sqrt(update_squares)], axis=1)
+    outputs = [loss, grad_norm]
+    for member in range(4):
+        outputs += [
+            renewed[member],
+            moved[member][0],
+            moved[member][1],
+            renewed[member].astype(jnp.bfloat16),
+        ]
+    return tuple(outputs) + (norms,)
+
+
 def solution(mesh):
+    body = fast_local if tree_fits(mesh) else plain_local
     in_specs = (
         P(("dp", "fsdp"), None, None),
         P(("dp", "fsdp"), None, None),
@@ -501,4 +1415,4 @@
         P(("dp", "fsdp")),
         P(),
     )
-    return jax.shard_map(local, mesh=mesh, in_specs=in_specs, out_specs=out_specs, check_vma=False)
+    return jax.shard_map(body, mesh=mesh, in_specs=in_specs, out_specs=out_specs, check_vma=False)

time: 3740 us -> 1990 us (0.53)
  waiting for transfers between devices: 2570 us -> 78.6 us
  Pallas kernels: 0 us -> 1010 us
  blocking collectives: 205 us -> 0 us
  matrix products: 372 us -> 231 us
  starting transfers between devices: 0.46 us -> 81.4 us
    reduce_scatter x6 -> x0, waiting for transfers between devices: 1830 us -> none  [the longest x2 769 us: local(): lax.psum_scatter(grad_rows_full, ('dp', 'fsdp'), scatter_dimension=0, til...]
    pallas_call x0 -> x8, Pallas kernels: none -> 1010 us  [the longest x3 593 us: owner_sums(): pl.pallas_call(functools.partial(owner_sum_kernel, groups), out_shape=sha...]
    all_gather x2 -> x0, waiting for transfers between devices: 458 us -> none  [the longest x1 307 us: local(): lax.all_gather(rows_w.astype(jnp.bfloat16), ('dp', 'fsdp'), axis=1, tiled...]
    unnamed x14 -> x0, waiting for transfers between devices: 285 us -> none
    unnamed x377 -> x486, local copies, waits for them, and re-layouts: 173 us -> 38 us
    dot_general x15 -> x4, matrix products: 113 us -> 5.03 us  [collected_sample_embeddings(): lax.dot_general(left.reshape(-1, left.shape[-1]), right.reshape(-1, right...]
    dot_general x16 -> x4, matrix products: 96.7 us -> 9.87 us  [gram_crossing(): lax.dot_general(left, right, (((left.ndim - 1,), (1,)), ((), ())), prefer...]
    unnamed x2 -> x0, blocking collectives: 86 us -> none
  transfers between devices with their start and end apart: 11 -> 45, of which waited for: 11 -> 23; matrix products, arithmetic and copies ran while one was open for 9% -> 35% of each run, Pallas kernels for 0% -> 51%
where the time goes in v1:
time: 1990 us
  Pallas kernels  1010 us (51%)
  local copies, waits for them, and re-layouts  322 us (16%)
  other arithmetic  247 us (12%)
  matrix products  231 us (12%)
  starting transfers between devices  81.4 us (4%)
  waiting for transfers between devices  78.6 us (4%)
    pallas_call x3, Pallas kernels, owner_sums(): pl.pallas_call(functools.partial(owner_sum_kernel, groups), out_shape=sha...  593 us
    pallas_call x1, Pallas kernels, gather_all(): pl.pallas_call(functools.partial(gather_kernel, units, len(arrays)), out_...  404 us
    dot_general x42, matrix products, dot(): lax.dot_general(left, right, ((over[:1], over[1:]), batch), preferred_ele...  207 us
    ppermute x39, waiting for transfers between devices, swap(): return lax.ppermute(value, AXES, [(i, i ^ bit) for i in range(count)])  77 us
    ppermute x39, starting transfers between devices, swap(): return lax.ppermute(value, AXES, [(i, i ^ bit) for i in range(count)])  65.2 us
    gather x7, other arithmetic, spread(): misc_map = ratios[4 * blocks + misc_kind]  57.1 us
  transfers between devices with their start and end apart: 45, of which 23 were waited for; matrix products, arithmetic and copies ran while one was open for 35% of the time, Pallas kernels for 51%

profile of v1, /device:TPU:0, one launch (start us, length us, event | category | flops | bytes accessed | tf_op | source)
XLA Modules:
  0.0 1987.0 jit_solution(17208845784957669393)
XLA Ops:
  21.5 404.2 %gather_all.1 = (bf16[3,32,288,1152]{3,2,1,0:T(8,128)(2,1)}, bf16[3,32,144,1152]{3,2,1,0:T(8,128)(2,1)}, bf16[1,32,144,1152]{3,2,1,0:T(8,128)(2,1)S(1)}) custom-call(bf16[3,288,1152]{2,1,0:T(8,128)(2,1)S(1)} %get-tuple-element.173.refs_0_, bf16[3,144,1152]{2,1,0:T(8,128)(2,1)S(1)} %copy-done.2, bf16[1,144,1152]{2,1,0:T(8,128)(2,1)S(1)} %bitcast.457), custom_call_target="tpu_custom_call" | custom-call | tf_op jit(solution)/shard_map/gather_all/pallas_call | solution.py:671
  429.6 19.6 copy.338
  463.0 15.8 fusion.154
  478.8 20.7 %fusion.155 = (bf16[1,16,288,1152]{3,2,1,0:T(8,128)(2,1)}, bf16[1,16,288,1152]{3,2,1,0:T(8,128)(2,1)}, bf16[1,16,288,1152]{3,2,1,0:T(8,128)(2,1)}) fusion(bf16[3,32,288,1152]{3,2,1,0:T(8,128)(2,1)} %get-tuple-element.31), kind=kLoop, calls=%fused_computation.547 | loop fusion | bytes 63700992 | tf_op jit(solution)/shard_map/slice | solution.py:1031
  501.8 32.7 %fusion.156 = (bf16[1,32,144,1152]{3,2,1,0:T(8,128)(2,1)}, bf16[1,32,144,1152]{3,2,1,0:T(8,128)(2,1)}, bf16[1,32,144,1152]{3,2,1,0:T(8,128)(2,1)}) fusion(bf16[3,32,144,1152]{3,2,1,0:T(8,128)(2,1)} %get-tuple-element.33), kind=kLoop, calls=%fused_computation.548 | loop fusion | bytes 63700992 | tf_op jit(solution)/shard_map/slice | solution.py:1157
  562.5 14.0 multiply_convert_fusion.5
  576.5 11.5 fusion.164
  608.6 13.0 multiply_convert_fusion.4
  621.6 10.9 fusion.166
  655.0 8.3 slice_bitcast_fusion.6
  668.7 17.4 pad_add_fusion
  715.9 7.2 multiply_convert_fusion.3
  733.3 10.5 fusion.23
  786.6 7.6 compare_reduce_fusion.6
  794.2 7.8 compare_reduce_fusion.10
  802.0 7.6 compare_reduce_fusion.2
  809.5 7.6 compare_reduce_fusion.4
  817.1 8.0 compare_reduce_fusion
  825.0 7.6 compare_reduce_fusion.8
  873.1 7.8 fusion.176
  905.5 203.4 %owner_sums.5 = (f32[144,1152]{1,0:T(8,128)}, f32[288,1152]{1,0:T(8,128)}, f32[288,1152]{1,0:T(8,128)}) custom-call(bf16[16,2,144,322]{3,2,1,0:T(8,128)(2,1)} %bitcast.499, bf16[8,2,288,322]{3,2,1,0:T(8,128)(2,1)} %bitcast.500, bf16[8,2,288,322]{3,2,1,0:T(8,128)(2,1)} %bitcast.503, bf16[1,322,1152]{2,1,0:T(8,128)(2,1)} %fusion.80.refs_3_, ...), custom_call_target="tpu_custom_call" | custom-call | tf_op jit(solution)/shard_map/owner_sums/pallas_call | solution.py:882
  1123.2 14.5 collective-permute-start.23
  1158.5 11.6 fusion.16
  1229.2 12.2 fusion.9
  1331.2 189.4 %owner_sums.4 = (f32[144,1152]{1,0:T(8,128)}, f32[288,1152]{1,0:T(8,128)}, f32[288,1152]{1,0:T(8,128)}) custom-call(bf16[16,2,144,322]{3,2,1,0:T(8,128)(2,1)} %bitcast.497, bf16[8,2,288,322]{3,2,1,0:T(8,128)(2,1)} %bitcast.498, bf16[8,2,288,322]{3,2,1,0:T(8,128)(2,1)} %bitcast.502, bf16[1,322,1152]{2,1,0:T(8,128)(2,1)} %copy.385.refs_3_, ...), custom_call_target="tpu_custom_call" | custom-call | tf_op jit(solution)/shard_map/owner_sums/pallas_call | solution.py:882
  1538.4 200.7 %owner_sums.3 = (f32[144,1152]{1,0:T(8,128)}, f32[288,1152]{1,0:T(8,128)}, f32[288,1152]{1,0:T(8,128)}) custom-call(bf16[16,2,144,322]{3,2,1,0:T(8,128)(2,1)} %bitcast.496, bf16[8,2,288,322]{3,2,1,0:T(8,128)(2,1)} %bitcast.504, bf16[8,2,288,322]{3,2,1,0:T(8,128)(2,1)} %bitcast.501, bf16[1,322,1152]{2,1,0:T(8,128)(2,1)} %copy.380.refs_3_, ...), custom_call_target="tpu_custom_call" | custom-call | tf_op jit(solution)/shard_map/owner_sums/pallas_call | solution.py:882
  1747.6 14.7 collective-permute-start.28
  1800.1 26.2 %collective-permute-done.13 = bf16[2,2,144,1152]{3,2,1,0:T(8,128)(2,1)S(1)} collective-permute-done((bf16[2,2,144,1152]{3,2,1,0:T(8,128)(2,1)S(1)}, bf16[2,2,144,1152]{3,2,1,0:T(8,128)(2,1)S(1)}, u32[]{:S(2)}, u32[]{:S(2)}) %collective-permute-start.13) | collective-permute-done | bytes 1327136 | tf_op jit(solution)/shard_map/ppermute | solution.py:481
  1873.9 9.8 concatenate.369
  1901.4 11.5 multiply_reduce_fusion.3
  1964.1 11.1 fusion.58
  1975.3 9.2 fusion.142
  (924 shorter events, 619.0 us)
Async XLA Ops:
  1.5 1110.3 %collective-permute-start.20 = (f32[1,1]{0,1:T(1,128)}, f32[1,1]{0,1:T(1,128)}, u32[]{:S(2)}, u32[]{:S(2)}) collective-permute-start(f32[1,1]{0,1:T(1,128)} %bitcast.179), channel_id=1, source_target_pairs={{0,1},{1,0},{2,3},{3,2},{4,5},{5,4},{6,7},{7,6},{8,9},{9,8},{10,11... | collective-permute-start | bytes 20 | tf_op jit(solution)/shard_map/ppermute | solution.py:481
  633.8 487.5 %collective-permute-start = (bf16[1,1152]{1,0:T(2,128)(2,1)}, bf16[1,1152]{1,0:T(2,128)(2,1)}, u32[]{:S(2)}, u32[]{:S(2)}) collective-permute-start(bf16[1,1152]{1,0:T(2,128)(2,1)} %convert_element_type.657), channel_id=1, source_target_pairs={{0,1},{1,0},{2,3},{3,2},{4,5},{5,4},{6,7},{7,6},{8,9},{9,8},{10,11... | collective-permute-start | bytes 6920 | tf_op jit(solution)/shard_map/ppermute | solution.py:481
  651.4 1123.5 %collective-permute-start.11 = (bf16[12,144,322]{2,1,0:T(8,128)(2,1)}, bf16[12,144,322]{2,1,0:T(8,128)(2,1)}, u32[]{:S(2)}, u32[]{:S(2)}) collective-permute-start(bf16[12,144,322]{2,1,0:T(8,128)(2,1)} %dynamic-slice_bitcast_fusion), channel_id=1, source_target_pairs={{0,1},{1,0},{2,3},{3,2},{4,5},{5,4},{6,7},{7,6},{8,9},{9,8},{10,11... | collective-permute-start | bytes 3338504 | tf_op jit(solution)/shard_map/ppermute | solution.py:481
  783.4 991.6 %collective-permute-start.12 = (bf16[1,322,1152]{2,1,0:T(8,128)(2,1)}, bf16[1,322,1152]{2,1,0:T(8,128)(2,1)}, u32[]{:S(2)}, u32[]{:S(2)}) collective-permute-start(bf16[1,322,1152]{2,1,0:T(8,128)(2,1)} %bitcast.151.x_own), channel_id=1, source_target_pairs={{0,1},{1,0},{2,3},{3,2},{4,5},{5,4},{6,7},{7,6},{8,9},{9,8},{10,11... | collective-permute-start | bytes 2225672 | tf_op jit(solution)/shard_map/ppermute | solution.py:481
  1122.1 15.7 collective-permute-start.1
  1123.2 16.1 collective-permute-start.23
  1141.5 5.6 collective-permute-start.3
  1143.9 5.1 collective-permute-start.24
  1147.2 5.3 collective-permute-start.4
  1315.6 431.0 %collective-permute-start.30 = (f32[16,1152]{1,0:T(8,128)S(1)}, f32[16,1152]{1,0:T(8,128)S(1)}, u32[]{:S(2)}, u32[]{:S(2)}) collective-permute-start(f32[16,1152]{1,0:T(8,128)S(1)} %concatenate.368), channel_id=1, source_target_pairs={{0,1},{1,0},{2,3},{3,2},{4,5},{5,4},{6,7},{7,6},{8,9},{9,8},{10,11... | collective-permute-start | bytes 221192 | tf_op jit(solution)/shard_map/ppermute | solution.py:481
  1325.0 414.1 %collective-permute-start.25 = (f32[1,1152]{1,0:T(1,128)S(1)}, f32[1,1152]{1,0:T(1,128)S(1)}, u32[]{:S(2)}, u32[]{:S(2)}) collective-permute-start(f32[1,1152]{1,0:T(1,128)S(1)} %copy.406), channel_id=1, source_target_pairs={{0,1},{1,0},{2,3},{3,2},{4,5},{5,4},{6,7},{7,6},{8,9},{9,8},{10,11... | collective-permute-start | bytes 13832 | tf_op jit(solution)/shard_map/ppermute | solution.py:481
  1331.1 447.7 %collective-permute-start.5 = (bf16[2,2,144,1152]{3,2,0,1:T(8,128)(2,1)}, bf16[2,2,144,1152]{3,2,0,1:T(8,128)(2,1)}, u32[]{:S(2)}, u32[]{:S(2)}) collective-permute-start(bf16[2,2,144,1152]{3,2,0,1:T(8,128)(2,1)} %bitcast.452), channel_id=1, source_target_pairs={{0,1},{1,0},{2,3},{3,2},{4,5},{5,4},{6,7},{7,6},{8,9},{9,8},{10,11... | collective-permute-start | bytes 3981320 | tf_op jit(solution)/shard_map/ppermute | solution.py:481
  1742.9 4.8 collective-permute-start.27
  1746.5 15.8 collective-permute-start.31
  1747.6 22.4 %collective-permute-start.28 = (f32[8,1152]{1,0:T(8,128)S(1)}, f32[8,1152]{1,0:T(8,128)S(1)}, u32[]{:S(2)}, u32[]{:S(2)}) collective-permute-start(f32[8,1152]{1,0:T(8,128)S(1)} %maximum_select_fusion.7), channel_id=1, source_target_pairs={{0,8},{1,9},{2,10},{3,11},{4,12},{5,13},{6,14},{7,15},{8,0},{9,1},... | collective-permute-start | bytes 110600 | tf_op jit(solution)/shard_map/ppermute | solution.py:481
  1766.7 5.9 collective-permute-start.33
  1770.1 70.0 %collective-permute-start.29 = (f32[16,1152]{1,0:T(8,128)S(1)}, f32[16,1152]{1,0:T(8,128)S(1)}, u32[]{:S(2)}, u32[]{:S(2)}) collective-permute-start(f32[16,1152]{1,0:T(8,128)S(1)} %maximum_select_fusion.5), channel_id=1, source_target_pairs={{0,16},{1,17},{2,18},{3,19},{4,20},{5,21},{6,22},{7,23},{8,24},{9,... | collective-permute-start | bytes 221192 | tf_op jit(solution)/shard_map/ppermute | solution.py:481
  1772.7 71.8 %collective-permute-start.34 = (f32[16,1152]{1,0:T(8,128)S(1)}, f32[16,1152]{1,0:T(8,128)S(1)}, u32[]{:S(2)}, u32[]{:S(2)}) collective-permute-start(f32[16,1152]{1,0:T(8,128)S(1)} %add.1222), channel_id=1, source_target_pairs={{0,16},{1,17},{2,18},{3,19},{4,20},{5,21},{6,22},{7,23},{8,24},{9,... | collective-permute-start | bytes 221192 | tf_op jit(solution)/shard_map/ppermute | solution.py:481
  1778.1 17.0 collective-permute-start.15
  1780.6 17.9 collective-permute-start.6
  1787.1 39.2 %collective-permute-start.13 = (bf16[2,2,144,1152]{3,2,1,0:T(8,128)(2,1)S(1)}, bf16[2,2,144,1152]{3,2,1,0:T(8,128)(2,1)S(1)}, u32[]{:S(2)}, u32[]{:S(2)}) collective-permute-start(bf16[2,2,144,1152]{3,2,1,0:T(8,128)(2,1)S(1)} %bitcast.458), channel_id=1, source_target_pairs={{0,2},{1,3},{2,0},{3,1},{4,6},{5,7},{6,4},{7,5},{8,10},{9,11},{10,... | collective-permute-start | bytes 3981320 | tf_op jit(solution)/shard_map/ppermute | solution.py:481
  1795.2 34.7 %collective-permute-start.16 = (bf16[1,144,1152]{2,1,0:T(8,128)(2,1)S(1)}, bf16[1,144,1152]{2,1,0:T(8,128)(2,1)S(1)}, u32[]{:S(2)}, u32[]{:S(2)}) collective-permute-start(bf16[1,144,1152]{2,1,0:T(8,128)(2,1)S(1)} %fusion.46), channel_id=1, source_target_pairs={{0,2},{1,3},{2,0},{3,1},{4,6},{5,7},{6,4},{7,5},{8,10},{9,11},{10,... | collective-permute-start | bytes 995336 | tf_op jit(solution)/shard_map/ppermute | solution.py:481
  1798.7 31.4 %collective-permute-start.7 = (bf16[144,1152]{1,0:T(8,128)(2,1)S(1)}, bf16[144,1152]{1,0:T(8,128)(2,1)S(1)}, u32[]{:S(2)}, u32[]{:S(2)}) collective-permute-start(bf16[144,1152]{1,0:T(8,128)(2,1)S(1)} %dynamic-slice_bitcast_fusion.2), channel_id=1, source_target_pairs={{0,4},{1,5},{2,6},{3,7},{4,0},{5,1},{6,2},{7,3},{8,12},{9,13},{10,... | collective-permute-start | bytes 995336 | tf_op jit(solution)/shard_map/ppermute | solution.py:481
  1826.5 10.7 collective-permute-start.14
  1830.2 21.8 %collective-permute-start.10 = (bf16[144,1152]{1,0:T(8,128)(2,1)S(1)}, bf16[144,1152]{1,0:T(8,128)(2,1)S(1)}, u32[]{:S(2)}, u32[]{:S(2)}) collective-permute-start(bf16[144,1152]{1,0:T(8,128)(2,1)S(1)} %fusion.49), channel_id=1, source_target_pairs={{8,0},{9,1},{10,2},{11,3},{12,4},{13,5},{14,6},{15,7}} | collective-permute-start | bytes 995336 | tf_op jit(solution)/shard_map/ppermute | solution.py:491
  1831.5 36.3 %collective-permute-start.9 = (bf16[144,1152]{1,0:T(8,128)(2,1)S(1)}, bf16[144,1152]{1,0:T(8,128)(2,1)}, u32[]{:S(2)}, u32[]{:S(2)}) collective-permute-start(bf16[144,1152]{1,0:T(8,128)(2,1)S(1)} %fusion.49), channel_id=1, source_target_pairs={{16,0},{17,1},{18,2},{19,3},{20,4},{21,5},{22,6},{23,7}} | collective-permute-start | bytes 995336 | tf_op jit(solution)/shard_map/ppermute | solution.py:491
  1837.2 30.5 %collective-permute-start.8 = (bf16[144,1152]{1,0:T(8,128)(2,1)S(1)}, bf16[144,1152]{1,0:T(8,128)(2,1)}, u32[]{:S(2)}, u32[]{:S(2)}) collective-permute-start(bf16[144,1152]{1,0:T(8,128)(2,1)S(1)} %fusion.49), channel_id=1, source_target_pairs={{24,0},{25,1},{26,2},{27,3},{28,4},{29,5},{30,6},{31,7}} | collective-permute-start | bytes 995336 | tf_op jit(solution)/shard_map/ppermute | solution.py:491
  1840.0 27.7 %collective-permute-start.17 = (bf16[144,1152]{1,0:T(8,128)(2,1)}, bf16[144,1152]{1,0:T(8,128)(2,1)}, u32[]{:S(2)}, u32[]{:S(2)}) collective-permute-start(bf16[144,1152]{1,0:T(8,128)(2,1)} %get-tuple-element.212), channel_id=1, source_target_pairs={{0,8},{1,9},{2,10},{3,11},{4,12},{5,13},{6,14},{7,15},{8,16},{9,17... | collective-permute-start | bytes 995336 | tf_op jit(solution)/shard_map/ppermute | solution.py:491
  1844.5 23.2 %collective-permute-start.18 = (bf16[144,1152]{1,0:T(8,128)(2,1)}, bf16[144,1152]{1,0:T(8,128)(2,1)}, u32[]{:S(2)}, u32[]{:S(2)}) collective-permute-start(bf16[144,1152]{1,0:T(8,128)(2,1)} %get-tuple-element.213), channel_id=1, source_target_pairs={{0,16},{1,17},{2,18},{3,19},{4,20},{5,21},{6,22},{7,23},{8,24},{9,... | collective-permute-start | bytes 995336 | tf_op jit(solution)/shard_map/ppermute | solution.py:491
  1852.0 15.8 collective-permute-start.19
  1895.5 4.4 collective-permute-start.39
  1941.7 4.4 collective-permute-start.44
  (244 other events, 2390.9 us)
